TPU v7x, 512 devices: a whole 4x8x8 slice. The times are simulated.
512 devices in a mesh: row: 64 (over y, x, z_hi), col: 8 (over z_lo, core).
Axes of the slice: x: 4, y: 8, z: 8 (z_hi: 2, z_lo: 4; z = z_hi * 4 + z_lo), core: 2. Of those that a mesh axis runs over, the one named last changes fastest.
Arguments:
- boundary_in: bfloat16 [2, 64, 8, 192, 768], P(None, 'row', 'col'), may hold values from -6 to 6
- site_tensors: bfloat16 [2, 64, 8, 2, 4, 4, 4, 4], P(None, 'row', 'col'), may hold values from -1.5 to 1.5
- spin_config: int32 [2, 64, 8], P(None, 'row', 'col'), may hold values from 0 to 1
- leg_charges: int32 [2, 64, 8, 4, 4], P(None, 'row', 'col'), may hold values from -1 to 1
- bond_charges: int32 [2, 64, 8, 192], P(None, 'row', 'col'), may hold values from -2 to 2
- left_proj: bfloat16 [2, 64, 8, 2, 192, 768], P(None, 'row', 'col'), may hold values from -0.4375 to 0.4375
- right_proj: bfloat16 [2, 64, 8, 2, 192, 768], P(None, 'row', 'col'), may hold values from -0.21875 to 0.21875
- proj_ranks: int32 [2, 64, 8, 2], P(None, 'row', 'col'), may hold values from 96 to 192
Outputs:
- boundary_out: bfloat16 [2, 64, 8, 192, 768], P(None, 'row', 'col')
All inputs are finite; a program needn't handle non-finite values.
Results may differ from a plain program's by a relative error of at most 0.008.
Values may be sent and summed in bfloat16 or wider, within the bound.
No kernel may reach another device: no remote copies, remote signals or barrier semaphores. Data moves between devices by JAX's collectives and lax.ppermute only.
A program may use at most 64 MiB of HBM per device.

v0:
```python
import jax
import jax.numpy as jnp
from jax import lax
from jax.sharding import PartitionSpec as P

eps = 1e-06


def passed_along(value, axis, steps):
    count = lax.axis_size(axis)
    pairs = [(source, (source + steps) % count) for source in range(count)]
    return lax.ppermute(value, axis, pairs)


def swapped(value, axis, distance):
    mask = 2**distance
    pairs = [(source, source ^ mask) for source in range(lax.axis_size(axis))]
    return lax.ppermute(value, axis, pairs)


def site_block(tensor, spin_value, leg_charge, toward_down):
    chosen = jnp.where(spin_value == 1, tensor[1], tensor[0])
    balance = (
        spin_value
        + leg_charge[0][:, None, None, None]
        + leg_charge[2][None, None, :, None]
        - leg_charge[1][None, :, None, None]
        - leg_charge[3][None, None, None, :]
    )
    masked = jnp.where(balance == 0, chosen, jnp.zeros_like(chosen))
    return jnp.where(toward_down, masked, jnp.transpose(masked, (0, 1, 3, 2)))


def mask_boundary(boundary, left_charge, incoming, right_charge):
    width = boundary.shape[0]
    legs = boundary.shape[1] // width
    shaped = boundary.reshape(width, legs, width)
    balance = left_charge[:, None, None] + incoming[None, :, None] - right_charge[None, None, :]
    return jnp.where(balance == 0, shaped, jnp.zeros_like(shaped))


def absorb(boundary, left_part, right_part, row_block, rank_from, rank_to):
    width = left_part.shape[0]
    legs = left_part.shape[1] // width
    positions = jnp.arange(width, dtype=jnp.int32)
    left_kept = jnp.where((positions < rank_from)[:, None], left_part, jnp.zeros_like(left_part))
    right_kept = jnp.where((positions < rank_to)[:, None], right_part, jnp.zeros_like(right_part))
    projected = jnp.dot(
        left_kept.reshape(width * legs, width),
        boundary.reshape(width, legs * width),
        preferred_element_type=jnp.float32,
    )
    projected = projected.astype(jnp.bfloat16).reshape(width, legs * legs, width)
    block_matrix = jnp.transpose(row_block, (3, 1, 0, 2)).reshape(legs * legs, legs * legs)
    combined = jnp.einsum(
        "yx,kxb->kyb", block_matrix, projected, preferred_element_type=jnp.float32
    ).astype(jnp.bfloat16)
    result = jnp.dot(
        combined.reshape(width * legs, legs * width),
        jnp.transpose(right_kept),
        preferred_element_type=jnp.float32,
    )
    return result.reshape(width, legs * width)


def normalize(values):
    return (values * lax.rsqrt(jnp.mean(values * values) + eps)).astype(jnp.bfloat16)


def local(
    boundary_in,
    site_tensors,
    spin_config,
    leg_charges,
    bond_charges,
    left_proj,
    right_proj,
    proj_ranks,
):
    top_first = lax.axis_index("row") % 2 == 0
    from_left = passed_along((bond_charges, proj_ranks), "col", 1)
    charge_left = jnp.concatenate([from_left[0], bond_charges[:, :, :-1]], axis=2)[:, 0]
    rank_left = jnp.concatenate([from_left[1], proj_ranks[:, :, :-1]], axis=2)[:, 0]
    boundary = boundary_in[:, 0]
    tensors = site_tensors[:, 0]
    spin_values = spin_config[:, 0]
    leg_values = leg_charges[:, 0]
    own_charge = bond_charges[:, 0]
    left_parts = left_proj[:, 0]
    right_parts = right_proj[:, 0]
    own_ranks = proj_ranks[:, 0]

    def first_step(
        given,
        tensor,
        spin_value,
        leg_charge,
        left_charge,
        right_charge,
        left_part,
        right_part,
        rank_from,
        rank_to,
    ):
        row_block = site_block(tensor, spin_value, leg_charge, top_first)
        incoming = jnp.where(top_first, leg_charge[2], leg_charge[3])
        cleaned = mask_boundary(given, left_charge, incoming, right_charge)
        return absorb(
            cleaned, left_part[0], right_part[0], row_block, rank_from[0], rank_to[0]
        ).astype(jnp.bfloat16)

    def second_step(
        received, tensor, spin_value, leg_charge, left_part, right_part, rank_from, rank_to
    ):
        row_block = site_block(tensor, spin_value, leg_charge, jnp.logical_not(top_first))
        return normalize(
            absorb(received, left_part[1], right_part[1], row_block, rank_from[1], rank_to[1])
        )

    first_all = jax.vmap(jax.vmap(first_step))
    second_all = jax.vmap(jax.vmap(second_step))
    halves = first_all(
        boundary,
        tensors,
        spin_values,
        leg_values,
        charge_left,
        own_charge,
        left_parts,
        right_parts,
        rank_left,
        own_ranks,
    )
    received = swapped(halves, "row", 0)
    finals = second_all(
        received, tensors, spin_values, leg_values, left_parts, right_parts, rank_left, own_ranks
    )
    return finals[:, None]


def solution(mesh):
    placed = (
        P(None, "row", "col", None, None),
        P(None, "row", "col", None, None, None, None, None),
        P(None, "row", "col"),
        P(None, "row", "col", None, None),
        P(None, "row", "col", None),
        P(None, "row", "col", None, None, None),
        P(None, "row", "col", None, None, None),
        P(None, "row", "col", None),
    )
    return jax.shard_map(
        local,
        mesh=mesh,
        in_specs=placed,
        out_specs=P(None, "row", "col", None, None),
        check_vma=False,
    )
```

profile of v0, /device:TPU:66, one launch (start us, length us, event | category | flops | bytes accessed | tf_op | source)
XLA Modules:
  0.0 94.2 jit_solution(15798003530995346393)
XLA Ops:
  0.0 0.0 copy-start.3
  0.0 2.0 %collective-permute-start.1 = (s32[2,1,1,192]{3,2,1,0:T(1,128)}, s32[2,1,1,192]{3,2,1,0:T(1,128)S(1)}, u32[]{:S(2)}, u32[]{:S(2)}) collective-permute-start(s32[2,1,1,192]{3,2,1,0:T(1,128)} %param.12), channel_id=1, source_target_pairs={{0,1},{1,2},{2,3},{3,4},{4,5},{5,6},{6,7},{7,0},{8,9},{9,10},{10,1... | collective-permute-start | bytes 4616 | tf_op jit(solution)/shard_map/ppermute | solution.py:12
  2.0 4.4 %collective-permute-start = (s32[2,1,1,2]{3,2,1,0:T(1,128)}, s32[2,1,1,2]{3,2,1,0:T(1,128)S(1)}, u32[]{:S(2)}, u32[]{:S(2)}) collective-permute-start(s32[2,1,1,2]{3,2,1,0:T(1,128)} %param.15), channel_id=1, source_target_pairs={{0,1},{1,2},{2,3},{3,4},{4,5},{5,6},{6,7},{7,0},{8,9},{9,10},{10,1... | collective-permute-start | bytes 56 | tf_op jit(solution)/shard_map/ppermute | solution.py:12
  6.4 0.7 copy.34
  7.1 0.8 fusion.35
  8.0 0.7 broadcast_compare_fusion
  8.6 0.7 broadcast_add_fusion.2
  9.4 0.1 broadcast_add_fusion.1
  9.4 0.1 broadcast_subtract_fusion
  9.5 0.9 fusion.23
  10.4 0.3 copy.16
  10.7 1.5 %fusion.26 = (bf16[2,1,4,4,4,4]{2,5,3,4,0,1:T(4,128)(2,1)}, bf16[2,1,4,4,4,4]{2,5,3,4,0,1:T(4,128)(2,1)S(1)}) fusion(bf16[2,1,4,4,4,4]{4,5,3,2,0,1:T(4,128)(2,1)S(1)} %copy.16, pred[]{:T(512)S(6)} %not.3, pred[]{:T(512)S(6)} %eq.34, bf16[2,1,2,4,4,4,4]{6,5,4,3,2,0,1:T(4,128)(2,1)} %bitcast.109, pred[2]{0:T(512)(128)(4,1)S(1)} %broadcast_compare_fusion, ...), kind=kLoop, calls=%fused_computation.39 | loop fusion | flops 3072 | bytes 5668 | tf_op jit(solution)/shard_map/vmap(vmap())/transpose | solution.py:54
  12.2 0.3 copy.17
  12.6 0.1 reshape.365
  12.7 2.1 %fusion.34 = (bf16[2,1,1,192,768]{4,3,2,0,1:T(8,128)(2,1)S(1)}, bf16[2,1,1,192,768]{4,3,2,0,1:T(8,128)(2,1)}) fusion(bf16[2,1,2,192,768]{4,3,2,0,1:T(8,128)(2,1)} %bitcast.107), kind=kLoop, calls=%fused_computation.63 | loop fusion | bytes 2359296 | tf_op jit(solution)/shard_map/vmap(vmap())/slice | solution.py:109
  14.8 0.7 squeeze.58
  15.6 0.1 sub.84
  15.7 0.0 copy-done.3
  15.7 0.2 slice_reduce_fusion
  15.8 0.7 iota_compare_fusion
  16.5 0.0 collective-permute-done
  16.5 0.2 slice_reduce_fusion.2
  16.7 0.7 iota_compare_fusion.2
  17.3 0.1 broadcast_in_dim.78
  17.5 0.7 broadcast_in_dim.79
  18.2 0.0 collective-permute-done.1
  18.2 0.1 broadcast_add_fusion
  18.3 0.6 sub.80
  18.9 1.0 %sub.81 = s32[2,192,768]{2,1,0:T(8,128)S(1)} reshape(s32[2,192,4,192]{3,2,1,0:T(4,128)S(1)} %sub.80) | data formatting | bytes 2359296 | tf_op jit(solution)/shard_map/vmap(vmap())/sub | solution.py:38
  19.9 3.3 %convolution_convert_fusion.1 = bf16[2,768,768]{2,1,0:T(8,128)(2,1)} fusion(bf16[2,768,192]{2,1,0:T(8,128)(2,1)S(1)} %squeeze.58, pred[2,768]{1,0:T(4,128)(4,1)} %broadcast_in_dim.79, s32[2,192,768]{2,1,0:T(8,128)S(1)} %sub.81, bf16[2,1,1,192,768]{4,3,2,1,0:T(8,128)(2,1)} %param.8, s32[2,768]{1,0:T(2,128)S(1)} %sub.84), kind=kOutput, calls=%fused_computation.3 | convolution fusion | flops 455344128 | bytes 4726272 | tf_op jit(solution)/shard_map/vmap(vmap())/dot_general | solution.py:48
  23.3 5.1 %reshape.357 = bf16[2,192,16,192]{3,2,1,0:T(8,128)(2,1)S(1)} reshape(bf16[2,768,768]{2,1,0:T(8,128)(2,1)} %convolution_convert_fusion.1) | data formatting | bytes 4718592 | tf_op jit(solution)/shard_map/reshape.32
  28.4 2.6 %convert_bitcast_fusion.1 = bf16[2,1,192,16,192]{4,3,2,0,1:T(8,128)(2,1)} fusion(bf16[2,192,16,192]{3,2,1,0:T(8,128)(2,1)S(1)} %reshape.357, bf16[2,16,16,1]{2,1,0,3:T(8,128)(2,1)S(1)} %reshape.365), kind=kOutput, calls=%fused_computation.1 | convolution fusion | flops 38928384 | bytes 4719616 | tf_op jit(solution)/shard_map/vmap(vmap(yx,kxb->kyb))/dot_general | solution.py:55
  31.0 0.0 copy-start.5
  31.0 5.3 %reshape.359 = bf16[2,768,768]{2,1,0:T(8,128)(2,1)S(1)} reshape(bf16[2,1,192,16,192]{4,3,2,0,1:T(8,128)(2,1)} %convert_bitcast_fusion.1) | data formatting | bytes 4718592 | tf_op jit(solution)/shard_map/reshape.37
  36.2 0.0 copy-done.5
  36.2 2.0 %convolution_convert_fusion.2 = bf16[2,768,192]{1,2,0:T(8,128)(2,1)S(1)} fusion(bf16[2,768,768]{2,1,0:T(8,128)(2,1)S(1)} %reshape.359, bf16[2,1,2,192,768]{4,3,2,0,1:T(8,128)(2,1)} %bitcast.123, pred[2,192]{1,0:T(4,128)(4,1)S(1)} %copy-done.5), kind=kOutput, calls=%fused_computation.4 | convolution fusion | flops 453574656 | bytes 3539328 | tf_op jit(solution)/shard_map/vmap(vmap())/dot_general | solution.py:58
  38.2 0.0 copy-start
  38.2 0.0 copy-start.1
  38.3 0.0 copy-start.2
  38.3 0.3 copy.19
  38.5 0.8 convert_element_type.57
  39.3 9.3 %collective-permute-start.2 = (bf16[2,1,192,768]{3,2,0,1:T(8,128)(2,1)S(1)}, bf16[2,1,192,768]{3,2,0,1:T(8,128)(2,1)S(1)}, u32[]{:S(2)}, u32[]{:S(2)}) collective-permute-start(bf16[2,1,192,768]{3,2,0,1:T(8,128)(2,1)S(1)} %convert_element_type.57), channel_id=1, source_target_pairs={{0,8},{8,0},{16,24},{24,16},{32,40},{40,32},{48,56},{56,48},{64,72... | collective-permute-start | bytes 1769480 | tf_op jit(solution)/shard_map/ppermute | solution.py:18
  48.6 0.0 copy-done
  48.6 0.7 squeeze.57
  49.4 0.0 copy-done.1
  49.4 0.3 copy.21
  49.7 0.1 reshape.366
  49.8 0.0 copy-done.2
  49.8 0.1 broadcast_in_dim.74
  50.0 0.2 broadcast_in_dim.75
  50.1 24.6 %collective-permute-done.2 = bf16[2,1,192,768]{3,2,0,1:T(8,128)(2,1)S(1)} collective-permute-done((bf16[2,1,192,768]{3,2,0,1:T(8,128)(2,1)S(1)}, bf16[2,1,192,768]{3,2,0,1:T(8,128)(2,1)S(1)}, u32[]{:S(2)}, u32[]{:S(2)}) %collective-permute-start.2) | collective-permute-done | bytes 589856 | tf_op jit(solution)/shard_map/ppermute | solution.py:18
  74.7 2.2 %convolution_convert_fusion = bf16[2,768,768]{2,1,0:T(8,128)(2,1)} fusion(bf16[2,768,192]{2,1,0:T(8,128)(2,1)S(1)} %squeeze.57, pred[2,768]{1,0:T(4,128)(4,1)S(1)} %broadcast_in_dim.75, bf16[2,1,192,768]{3,2,0,1:T(8,128)(2,1)S(1)} %collective-permute-done.2), kind=kOutput, calls=%fused_computation.2 | convolution fusion | flops 454459392 | bytes 3540480 | tf_op jit(solution)/shard_map/vmap(vmap())/dot_general | solution.py:48
  77.0 5.1 %reshape.361 = bf16[2,192,16,192]{3,2,1,0:T(8,128)(2,1)S(1)} reshape(bf16[2,768,768]{2,1,0:T(8,128)(2,1)} %convolution_convert_fusion) | data formatting | bytes 4718592 | tf_op jit(solution)/shard_map/reshape.44
  82.1 2.6 %convert_bitcast_fusion = bf16[2,1,192,16,192]{4,3,2,0,1:T(8,128)(2,1)} fusion(bf16[2,192,16,192]{3,2,1,0:T(8,128)(2,1)S(1)} %reshape.361, bf16[2,16,16,1]{2,1,0,3:T(8,128)(2,1)S(1)} %reshape.366), kind=kOutput, calls=%fused_computation | convolution fusion | flops 38928384 | bytes 4719616 | tf_op jit(solution)/shard_map/vmap(vmap(yx,kxb->kyb))/dot_general | solution.py:55
  84.7 0.0 copy-start.4
  84.7 5.3 %reshape.363 = bf16[2,768,768]{2,1,0:T(8,128)(2,1)S(1)} reshape(bf16[2,1,192,16,192]{4,3,2,0,1:T(8,128)(2,1)} %convert_bitcast_fusion) | data formatting | bytes 4718592 | tf_op jit(solution)/shard_map/reshape.49
  89.9 0.0 copy-done.4
  89.9 2.1 %multiply_reduce_fusion = (f32[2]{0:T(128)S(1)}, f32[2,768,192]{1,2,0:T(8,128)S(1)}) fusion(bf16[2,768,768]{2,1,0:T(8,128)(2,1)S(1)} %reshape.363, bf16[2,1,2,192,768]{4,3,2,0,1:T(8,128)(2,1)} %bitcast.124, pred[2,192]{1,0:T(4,128)(4,1)S(1)} %copy-done.4), kind=kOutput, calls=%fused_computation.6 | convolution fusion | flops 453869568 | bytes 4129160 | tf_op jit(solution)/shard_map/vmap(vmap())/dot_general | solution.py:58
  92.1 0.5 copy.22
  92.5 0.6 reshape.364
  93.2 1.0 %fusion.6 = bf16[2,1,1,192,768]{4,3,2,1,0:T(8,128)(2,1)} fusion(f32[2,1,1,192,768]{4,3,0,2,1:T(8,128)S(1)} %reshape.364, f32[2]{0:T(128)S(1)} %add_rsqrt_fusion), kind=kLoop, calls=%fused_computation.13 | loop fusion | flops 589824 | bytes 1769480 | tf_op jit(solution)/shard_map/vmap(vmap())/convert_element_type | solution.py:67
  (4 shorter events, 0.0 us)
Async XLA Ops:
  0.0 15.7 %copy-start.3 = (s32[2,1,1,2]{3,2,1,0:T(1,128)S(1)}, s32[2,1,1,2]{3,2,1,0:T(1,128)}, u32[]{:S(2)}) copy-start(s32[2,1,1,2]{3,2,1,0:T(1,128)} %param.15) | copy-start | bytes 52
  0.0 18.2 %collective-permute-start.1 = (s32[2,1,1,192]{3,2,1,0:T(1,128)}, s32[2,1,1,192]{3,2,1,0:T(1,128)S(1)}, u32[]{:S(2)}, u32[]{:S(2)}) collective-permute-start(s32[2,1,1,192]{3,2,1,0:T(1,128)} %param.12), channel_id=1, source_target_pairs={{0,1},{1,2},{2,3},{3,4},{4,5},{5,6},{6,7},{7,0},{8,9},{9,10},{10,1... | collective-permute-start | bytes 4616 | tf_op jit(solution)/shard_map/ppermute | solution.py:12
  2.0 14.5 %collective-permute-start = (s32[2,1,1,2]{3,2,1,0:T(1,128)}, s32[2,1,1,2]{3,2,1,0:T(1,128)S(1)}, u32[]{:S(2)}, u32[]{:S(2)}) collective-permute-start(s32[2,1,1,2]{3,2,1,0:T(1,128)} %param.15), channel_id=1, source_target_pairs={{0,1},{1,2},{2,3},{3,4},{4,5},{5,6},{6,7},{7,0},{8,9},{9,10},{10,1... | collective-permute-start | bytes 56 | tf_op jit(solution)/shard_map/ppermute | solution.py:12
  31.0 5.3 %copy-start.5 = (pred[2,192]{1,0:T(4,128)(4,1)S(1)}, pred[2,192]{1,0:T(4,128)(4,1)}, u32[]{:S(2)}) copy-start(pred[2,192]{1,0:T(4,128)(4,1)} %get-tuple-element.22) | copy-start | bytes 1156
  38.2 10.4 %copy-start = (bf16[2,1,1,192,768]{4,3,2,0,1:T(8,128)(2,1)S(1)}, bf16[2,1,1,192,768]{4,3,2,0,1:T(8,128)(2,1)}, u32[]{:S(2)}) copy-start(bf16[2,1,1,192,768]{4,3,2,0,1:T(8,128)(2,1)} %get-tuple-element.10) | copy-start | bytes 1769476
  38.2 11.1 %copy-start.1 = (bf16[2,1,4,4,4,4]{2,5,3,4,0,1:T(4,128)(2,1)S(1)}, bf16[2,1,4,4,4,4]{2,5,3,4,0,1:T(4,128)(2,1)}, u32[]{:S(2)}) copy-start(bf16[2,1,4,4,4,4]{2,5,3,4,0,1:T(4,128)(2,1)} %get-tuple-element.11) | copy-start | bytes 3076
  38.3 11.6 %copy-start.2 = (pred[2,192]{1,0:T(4,128)(4,1)S(1)}, pred[2,192]{1,0:T(4,128)(4,1)}, u32[]{:S(2)}) copy-start(pred[2,192]{1,0:T(4,128)(4,1)} %get-tuple-element.20) | copy-start | bytes 1156
  39.3 35.4 %collective-permute-start.2 = (bf16[2,1,192,768]{3,2,0,1:T(8,128)(2,1)S(1)}, bf16[2,1,192,768]{3,2,0,1:T(8,128)(2,1)S(1)}, u32[]{:S(2)}, u32[]{:S(2)}) collective-permute-start(bf16[2,1,192,768]{3,2,0,1:T(8,128)(2,1)S(1)} %convert_element_type.57), channel_id=1, source_target_pairs={{0,8},{8,0},{16,24},{24,16},{32,40},{40,32},{48,56},{56,48},{64,72... | collective-permute-start | bytes 1769480 | tf_op jit(solution)/shard_map/ppermute | solution.py:18
  84.7 5.3 %copy-start.4 = (pred[2,192]{1,0:T(4,128)(4,1)S(1)}, pred[2,192]{1,0:T(4,128)(4,1)}, u32[]{:S(2)}) copy-start(pred[2,192]{1,0:T(4,128)(4,1)} %get-tuple-element.21) | copy-start | bytes 1156
where the time goes:
time: 95 us; the launch traced here: 94.2 us
  local copies, waits for them, and re-layouts  32.3 us (34%)
  waiting for transfers between devices  24.6 us (26%)
  starting transfers between devices  15.7 us (17%)
  matrix products  14.9 us (16%)
  other arithmetic  6.35 us (7%)
    ppermute x1, waiting for transfers between devices, swapped(): return lax.ppermute(value, axis, pairs)  24.6 us
    another operation x6, local copies, waits for them, and re-layouts  20.9 us
    ppermute x1, starting transfers between devices, swapped(): return lax.ppermute(value, axis, pairs)  9.3 us
    ppermute x2, starting transfers between devices, passed_along(): return lax.ppermute(value, axis, pairs)  6.42 us
    dot_general x2, matrix products, absorb(): jnp.dot(left_kept.reshape(width * legs, width), boundary.reshape(width, l...  5.56 us
    dot_general x2, matrix products, absorb(): jnp.einsum('yx,kxb->kyb', block_matrix, projected, preferred_element_type...  5.2 us
    dot_general x2, matrix products, absorb(): jnp.dot(combined.reshape(width * legs, legs * width), jnp.transpose(right...  4.14 us
    slice x1, local copies, waits for them, and re-layouts, first_step(): left_part[0]  2.14 us
  transfers between devices with their start and end apart: 3, of which 1 were waited for; matrix products, arithmetic and copies ran while one was open for 14% of the time, Pallas kernels for 0%

commit v1 on v0

v1 whole, which is shorter than its diff:
```python
import functools

import jax
import jax.numpy as jnp
from jax import lax
from jax.experimental import pallas as pl
from jax.experimental.pallas import tpu as pltpu
from jax.sharding import PartitionSpec as P

eps = 1e-06
VMEM_BYTES = 32 * 1024 * 1024
GROUP = 16
LANES = 128


def passed_along(value, axis, steps):
    count = lax.axis_size(axis)
    pairs = [(source, (source + steps) % count) for source in range(count)]
    return lax.ppermute(value, axis, pairs)


def swapped(value, axis, distance):
    mask = 2**distance
    pairs = [(source, source ^ mask) for source in range(lax.axis_size(axis))]
    return lax.ppermute(value, axis, pairs)


def padded(width):
    return -(-width // LANES) * LANES


def pick(index, values):
    out = jnp.zeros_like(index)
    for j, value in enumerate(values):
        out = jnp.where(index == j, value, out)
    return out


def expand_block(s, legs, natural, site_ref, spin_ref, leg_ref, by_left_ref, by_right_ref, kron_ref):
    squared = legs * legs
    spin = spin_ref[0, 0, s]
    leg = [[leg_ref[s, 0, 0, j, t] for t in range(legs)] for j in range(4)]
    for l in range(legs):
        for e in range(legs):
            tile = jnp.where(spin == 1, site_ref[s, 0, 0, 1, l, e], site_ref[s, 0, 0, 0, l, e])
            tile = tile.astype(jnp.float32)
            by_left_ref[l * legs : (l + 1) * legs, e * legs : (e + 1) * legs] = tile
            by_right_ref[e * legs : (e + 1) * legs, l * legs : (l + 1) * legs] = tile
    turned = jnp.transpose(by_left_ref[...])[:squared, :squared]
    entries = jnp.where(natural, turned, by_right_ref[:squared, :squared])
    row = lax.broadcasted_iota(jnp.int32, (squared, squared), 0)
    col = lax.broadcasted_iota(jnp.int32, (squared, squared), 1)
    right, outer, left, inner = row // legs, row % legs, col // legs, col % legs
    up, down = jnp.where(natural, inner, outer), jnp.where(natural, outer, inner)
    balance = spin + pick(left, leg[0]) + pick(up, leg[2]) - pick(right, leg[1]) - pick(down, leg[3])
    entries = jnp.where(balance == 0, entries, 0.0).astype(jnp.bfloat16)
    size = squared * GROUP
    tall = lax.broadcasted_iota(jnp.int32, (size, squared), 0) // GROUP
    tall = (tall == lax.broadcasted_iota(jnp.int32, (size, squared), 1)).astype(jnp.bfloat16)
    wide = lax.broadcasted_iota(jnp.int32, (squared, size), 1) // GROUP
    wide = (wide == lax.broadcasted_iota(jnp.int32, (squared, size), 0)).astype(jnp.bfloat16)
    spread = jnp.dot(tall, entries, preferred_element_type=jnp.float32).astype(jnp.bfloat16)
    spread = jnp.dot(spread, wide, preferred_element_type=jnp.float32)
    row = lax.broadcasted_iota(jnp.int32, (size, size), 0)
    col = lax.broadcasted_iota(jnp.int32, (size, size), 1)
    kron_ref[...] = jnp.where(row % GROUP == col % GROUP, spread, 0.0).astype(jnp.bfloat16)


def stack_left(legs, width, left_ref, stack_ref):
    for l in range(legs):
        stack_ref[l * width : (l + 1) * width, :] = left_ref[:, l * width : (l + 1) * width]


def turn_right(legs, width, rank, right_ref, turned_ref):
    wide = padded(width)
    kept = lax.broadcasted_iota(jnp.int32, (width, width), 1) < rank
    for e in range(legs):
        turned = jnp.transpose(right_ref[:, e * width : (e + 1) * width])
        turned_ref[e * wide : e * wide + width, :] = jnp.where(kept, turned, jnp.zeros_like(turned))
        if wide > width:
            turned_ref[e * wide + width : (e + 1) * wide, :] = jnp.zeros((wide - width, width), jnp.bfloat16)


def absorb(legs, width, given, stack_ref, kron_ref, turned_ref, spaced_ref, proj_ref, comb_ref):
    wide = padded(width)
    for i in range(legs):
        spaced_ref[:, i * wide : i * wide + width] = given[:, i * width : (i + 1) * width]
        if wide > width:
            spaced_ref[:, i * wide + width : (i + 1) * wide] = jnp.zeros((width, wide - width), jnp.bfloat16)
    for l in range(legs):
        proj = jnp.dot(stack_ref[l * width : (l + 1) * width, :], spaced_ref[...], preferred_element_type=jnp.float32)
        proj_ref[l * width : (l + 1) * width, :] = proj.astype(jnp.bfloat16)
    for q in range(width // GROUP):
        part = jnp.concatenate(
            [
                proj_ref[l * width + q * GROUP : l * width + (q + 1) * GROUP, i * wide : (i + 1) * wide]
                for l in range(legs)
                for i in range(legs)
            ],
            axis=0,
        )
        comb = jnp.dot(kron_ref[...], part, preferred_element_type=jnp.float32).astype(jnp.bfloat16)
        for e in range(legs):
            for o in range(legs):
                place = (e * legs + o) * GROUP
                comb_ref[o * width + q * GROUP : o * width + (q + 1) * GROUP, e * wide : (e + 1) * wide] = (
                    comb[place : place + GROUP, :]
                )
    return jnp.dot(comb_ref[...], turned_ref[...], preferred_element_type=jnp.float32)


def prepare(
    s, step, legs, width, top_first,
    spin_in, leg_in, rank_in, site_in, left_in, right_in,
    stack_ref, kron_ref, turned_ref,
    spin_ref, leg_ref, rank_ref, site_ref, left_ref, right_ref, by_left_ref, by_right_ref, sems,
):
    copies = [
        pltpu.make_async_copy(source, target, sems.at[j])
        for j, (source, target) in enumerate(
            [(spin_in, spin_ref), (leg_in, leg_ref), (rank_in, rank_ref), (site_in, site_ref),
             (right_in.at[s, 0, 0, step], right_ref), (left_in.at[s, 0, 0, step], left_ref)]
        )
    ]
    for copy in copies:
        copy.start()
    for copy in copies[:4]:
        copy.wait()
    natural = top_first if step == 0 else jnp.logical_not(top_first)
    expand_block(s, legs, natural, site_ref, spin_ref, leg_ref, by_left_ref, by_right_ref, kron_ref)
    copies[4].wait()
    turn_right(legs, width, rank_ref[s, 0, 0, step], right_ref, turned_ref)
    copies[5].wait()
    stack_left(legs, width, left_ref, stack_ref)


def rows_kept(s, step, width, from_left_ref):
    rank = from_left_ref[s, 0, :, width + step : width + step + 1]
    return lax.broadcasted_iota(jnp.int32, (width, 1), 0) < rank


def is_top_first():
    return lax.rem(lax.axis_index("row"), 2) == 0


def put_half(s, legs, width, from_left_ref, result, half_ref):
    kept = rows_kept(s, 0, width, from_left_ref)
    for o in range(legs):
        part = jnp.where(kept, result[o * width : (o + 1) * width], 0.0)
        half_ref[0, :, o * width : (o + 1) * width] = part.astype(jnp.bfloat16)


def prepare_first_kernel(
    s, legs, width,
    spin_in, leg_in, rank_in, site_in, charge_in, given_in, left_in, right_in,
    stack_ref, kron_ref, turned_ref, given_ref, charge_ref, leg_out_ref,
    *scratch,
):
    *scratch, more = scratch
    fetch_given = pltpu.make_async_copy(given_in.at[s, 0, 0], given_ref, more.at[0])
    fetch_charge = pltpu.make_async_copy(charge_in, charge_ref, more.at[1])
    fetch_given.start()
    fetch_charge.start()
    prepare(
        s, 0, legs, width, is_top_first(),
        spin_in, leg_in, rank_in, site_in, left_in, right_in, stack_ref, kron_ref, turned_ref, *scratch,
    )
    leg_ref = scratch[1]
    for i in range(legs):
        incoming = jnp.where(is_top_first(), leg_ref[s, 0, 0, 2, i], leg_ref[s, 0, 0, 3, i])
        leg_out_ref[i : i + 1, :] = jnp.full((1, LANES), incoming, jnp.int32)
    fetch_given.wait()
    fetch_charge.wait()


def first_kernel(
    s, legs, width,
    from_left_ref, stack_ref, kron_ref, turned_ref, given_ref, charge_ref, incoming_ref,
    half_ref, spaced_ref, proj_ref, comb_ref,
):
    row_charge = from_left_ref[s, 0, :, :width].astype(jnp.float32)
    left_charge = jnp.transpose(jnp.broadcast_to(row_charge, (LANES, width)))[:, :1]
    right_charge = charge_ref[s, 0].astype(jnp.float32)
    wanted = [right_charge - incoming_ref[i : i + 1, :1].astype(jnp.float32) for i in range(legs)]
    given = given_ref[...]
    given = jnp.where(left_charge == jnp.concatenate(wanted, axis=1), given, jnp.zeros_like(given))
    result = absorb(legs, width, given, stack_ref, kron_ref, turned_ref, spaced_ref, proj_ref, comb_ref)
    put_half(s, legs, width, from_left_ref, result, half_ref)


def whole_first_kernel(
    s, legs, width,
    from_left_ref, _after, spin_in, leg_in, rank_in, site_in, charge_in, given_in, left_in, right_in,
    half_ref,
    stack_ref, kron_ref, turned_ref, given_ref, charge_ref, incoming_ref, spaced_ref, proj_ref, comb_ref,
    *scratch,
):
    prepare_first_kernel(
        s, legs, width,
        spin_in, leg_in, rank_in, site_in, charge_in, given_in, left_in, right_in,
        stack_ref, kron_ref, turned_ref, given_ref, charge_ref, incoming_ref, *scratch,
    )
    first_kernel(
        s, legs, width,
        from_left_ref, stack_ref, kron_ref, turned_ref, given_ref, charge_ref, incoming_ref,
        half_ref, spaced_ref, proj_ref, comb_ref,
    )


def prepare_second_kernel(
    s, legs, width, _after, spin_in, leg_in, rank_in, site_in, left_in, right_in,
    stack_ref, kron_ref, turned_ref, *scratch,
):
    prepare(
        s, 1, legs, width, is_top_first(),
        spin_in, leg_in, rank_in, site_in, left_in, right_in, stack_ref, kron_ref, turned_ref, *scratch,
    )


def second_kernel(
    s, legs, width, from_left_ref, received_ref, stack_ref, kron_ref, turned_ref, *rest,
):
    out_ref, spaced_ref, proj_ref, comb_ref, final_ref, sem = rest[-6:]
    result = absorb(
        legs, width, received_ref[0], stack_ref, kron_ref, turned_ref, spaced_ref, proj_ref, comb_ref
    )
    kept = rows_kept(s, 1, width, from_left_ref)
    parts = [jnp.where(kept, result[o * width : (o + 1) * width], 0.0) for o in range(legs)]
    total = sum(jnp.sum(part * part, axis=0, keepdims=True) for part in parts)
    mean = jnp.sum(total, axis=1, keepdims=True) * (1.0 / result.size)
    scale = lax.rsqrt(mean + eps)
    for o in range(legs):
        final_ref[:, o * width : (o + 1) * width] = (parts[o] * scale).astype(jnp.bfloat16)
    copy = pltpu.make_async_copy(final_ref, out_ref.at[s, 0, 0], sem)
    copy.start()
    copy.wait()


def local(
    boundary_in,
    site_tensors,
    spin_config,
    leg_charges,
    bond_charges,
    left_proj,
    right_proj,
    proj_ranks,
):
    states, width, legs = boundary_in.shape[0], boundary_in.shape[3], site_tensors.shape[4]
    squared, long, wide = legs * legs, legs * width, padded(width)
    size = squared * GROUP
    vmem = pl.BlockSpec(memory_space=pltpu.VMEM)
    hbm = pl.BlockSpec(memory_space=pltpu.HBM)
    bf16, i32 = jnp.bfloat16, jnp.int32

    edge = jnp.concatenate([bond_charges, proj_ranks], axis=3)
    from_left = passed_along(edge, "col", 1)

    ready_shapes = [((legs * width, width), bf16), ((size, size), bf16), ((legs * wide, width), bf16)]
    given_shapes = [((width, long), bf16), (bond_charges.shape, i32), ((8, LANES), i32)]
    prepare_scratch = [
        pltpu.SMEM((1, 1, states), i32),
        pltpu.SMEM(leg_charges.shape, i32),
        pltpu.SMEM(proj_ranks.shape, i32),
        pltpu.VMEM(site_tensors.shape, bf16),
        pltpu.VMEM((width, long), bf16),
        pltpu.VMEM((width, long), bf16),
        pltpu.VMEM((LANES, LANES), jnp.float32),
        pltpu.VMEM((LANES, LANES), jnp.float32),
        pltpu.SemaphoreType.DMA((6,)),
    ]
    absorb_scratch = [
        pltpu.VMEM((width, legs * wide), bf16),
        pltpu.VMEM((legs * width, legs * wide), bf16),
        pltpu.VMEM((legs * width, legs * wide), bf16),
    ]
    flops = 2 * (2 * width * long * long + long * long * GROUP)

    def call(kernel, s, name, out_shapes, in_specs, scratch, cost, **options):
        return pl.pallas_call(
            functools.partial(kernel, s, legs, width),
            out_shape=[jax.ShapeDtypeStruct(*shape) for shape in out_shapes],
            in_specs=in_specs,
            scratch_shapes=scratch,
            compiler_params=pltpu.CompilerParams(vmem_limit_bytes=VMEM_BYTES),
            cost_estimate=pl.CostEstimate(flops=int(flops * cost), bytes_accessed=8 * width * long, transcendentals=0),
            name=name,
            **options,
        )

    spins = jnp.transpose(spin_config, (1, 2, 0))
    spins, leg_charges, proj_ranks, site_tensors, bond_charges, boundary_in, left_proj, right_proj = (
        pltpu.with_memory_space_constraint(value, pltpu.HBM)
        for value in (spins, leg_charges, proj_ranks, site_tensors, bond_charges, boundary_in, left_proj, right_proj)
    )
    small = (spins, leg_charges, proj_ranks, site_tensors)
    half_shape = ((1, width, long), bf16)
    ready = call(
        prepare_first_kernel, 0, "prepare_first", ready_shapes + given_shapes, [hbm] * 8,
        prepare_scratch + [pltpu.SemaphoreType.DMA((2,))], 1, out_specs=[vmem] * 6,
    )(*small, bond_charges, boundary_in, left_proj, right_proj)
    (half,) = call(
        first_kernel, 0, "first_absorption", [half_shape], [vmem] * 7, absorb_scratch, 1, out_specs=[vmem]
    )(from_left, *ready)
    halves = [half]
    for s in range(1, states):
        (half,) = call(
            whole_first_kernel, s, "whole_first_absorption", [half_shape], [vmem] + [hbm] * 9,
            [pltpu.VMEM(*shape) for shape in ready_shapes + given_shapes]
            + absorb_scratch + prepare_scratch + [pltpu.SemaphoreType.DMA((2,))], 1, out_specs=[vmem],
        )(from_left, halves[-1], *small, bond_charges, boundary_in, left_proj, right_proj)
        halves.append(half)
    received = [swapped(half, "row", 0) for half in halves]
    readies = [
        call(
            prepare_second_kernel, s, "prepare_second", ready_shapes, [hbm] * 7, prepare_scratch, 1,
            out_specs=[vmem] * 3,
        )(halves[-1], *small, left_proj, right_proj)
        for s in range(states)
    ]
    out = None
    for s in range(states):
        more = [] if out is None else [out]
        (out,) = call(
            second_kernel, s, "second_absorption", [(boundary_in.shape, bf16)], [vmem] * 5 + [hbm] * len(more),
            absorb_scratch + [pltpu.VMEM((width, long), bf16), pltpu.SemaphoreType.DMA], 1,
            out_specs=[hbm], input_output_aliases={5: 0} if more else {},
        )(from_left, received[s], *readies[s], *more)
    return out


def solution(mesh):
    placed = (
        P(None, "row", "col", None, None),
        P(None, "row", "col", None, None, None, None, None),
        P(None, "row", "col"),
        P(None, "row", "col", None, None),
        P(None, "row", "col", None),
        P(None, "row", "col", None, None, None),
        P(None, "row", "col", None, None, None),
        P(None, "row", "col", None),
    )
    return jax.shard_map(
        local,
        mesh=mesh,
        in_specs=placed,
        out_specs=P(None, "row", "col", None, None),
        check_vma=False,
    )
```

time: 95 us -> 52.5 us (0.55)
  the two profiles are of different devices: /device:TPU:66 before, /device:TPU:36 now
where the time goes in v1:
time: 52.5 us; the launch traced here: 52.3 us
  waiting for transfers between devices  22.2 us (42%)
  Pallas kernels  16.4 us (31%)
  starting transfers between devices  12.8 us (24%)
  other arithmetic  0.77 us (1%)
    ppermute x2, waiting for transfers between devices, swapped(): return lax.ppermute(value, axis, pairs)  17.4 us
    ppermute x2, starting transfers between devices, swapped(): return lax.ppermute(value, axis, pairs)  10.9 us
    pallas_call x2, Pallas kernels, local(): call(second_kernel, s, 'second_absorption', [(boundary_in.shape, bf16)],...  5.32 us
    ppermute x1, waiting for transfers between devices, passed_along(): return lax.ppermute(value, axis, pairs)  4.84 us
    pallas_call x1, Pallas kernels, local(): call(whole_first_kernel, s, 'whole_first_absorption', [half_shape], [vmem...  3.7 us
    pallas_call x2, Pallas kernels, local(): call(prepare_second_kernel, s, 'prepare_second', ready_shapes, [hbm] * 7,...  3.61 us
    ppermute x1, starting transfers between devices, passed_along(): return lax.ppermute(value, axis, pairs)  1.91 us
    pallas_call x1, Pallas kernels, local(): call(first_kernel, 0, 'first_absorption', [half_shape], [vmem] * 7, absor...  1.9 us
  transfers between devices with their start and end apart: 3, of which 3 were waited for; matrix products, arithmetic and copies ran while one was open for 0% of the time, Pallas kernels for 23%

profile of v1, /device:TPU:36, one launch (start us, length us, event | category | flops | bytes accessed | tf_op | source)
XLA Modules:
  0.0 52.3 jit_solution(9681257220451598555)
XLA Ops:
  0.0 0.8 %pad_add_fusion = s32[2,1,1,194]{3,2,1,0:T(1,128)S(1)} fusion(s32[2,1,1,2]{3,2,1,0:T(1,128)} %rank_in.7, s32[2,1,1,192]{3,2,1,0:T(1,128)} %charge_in.3), kind=kLoop, calls=%fused_computation | loop fusion | flops 388 | bytes 3104 | tf_op jit(solution)/shard_map/concatenate | solution.py:256
  0.8 1.9 %collective-permute-start = (s32[2,1,1,194]{3,2,1,0:T(1,128)S(1)}, s32[2,1,1,194]{3,2,1,0:T(1,128)S(1)}, u32[]{:S(2)}, u32[]{:S(2)}) collective-permute-start(s32[2,1,1,194]{3,2,1,0:T(1,128)S(1)} %pad_add_fusion), channel_id=1, source_target_pairs={{0,1},{1,2},{2,3},{3,4},{4,5},{5,6},{6,7},{7,0},{8,9},{9,10},{10,1... | collective-permute-start | bytes 4664 | tf_op jit(solution)/shard_map/ppermute | solution.py:19
  2.7 1.8 %prepare_first.1 = (bf16[768,192]{1,0:T(8,128)(2,1)S(1)}, bf16[256,256]{1,0:T(8,128)(2,1)S(1)}, bf16[1024,192]{1,0:T(8,128)(2,1)S(1)}, bf16[192,768]{1,0:T(8,128...) custom-call(s32[1,1,2]{2,1,0:T(1,128)} %bitcast.1, s32[2,1,1,4,4]{4,3,2,1,0:T(4,128)} %leg_in.7, ...), custom_call_target="tpu_custom_call" | custom-call | flops 471859200 | bytes 1179648 | tf_op jit(solution)/shard_map/prepare_first/pallas_call | solution.py:298
  4.5 4.8 %collective-permute-done.from_left_ref = s32[2,1,1,194]{3,2,1,0:T(1,128)S(1)} collective-permute-done((s32[2,1,1,194]{3,2,1,0:T(1,128)S(1)}, s32[2,1,1,194]{3,2,1,0:T(1,128)S(1)}, u32[]{:S(2)}, u32[]{:S(2)}) %collective-permute-start) | collective-permute-done | bytes 1584 | tf_op jit(solution)/shard_map/ppermute | solution.py:19
  9.4 1.9 %first_absorption.1._after = bf16[1,192,768]{2,1,0:T(8,128)(2,1)S(1)} custom-call(s32[2,1,1,194]{3,2,1,0:T(1,128)S(1)} %collective-permute-done.from_left_ref, bf16[768,192]{1,0:T(8,128)(2,1)S(1)} %get-tuple-element.17.stack_ref, bf16[256,256]{1,0:T(8,128)(2,1)S(1)} %get-tuple-element.18.kron_ref, bf16[1024,192]{1,0:T(8,128)(2,1)S(1)} %get-tuple-element.19.turned_ref, ...), custom_call_target="tpu_custom_call" | custom-call | flops 471859200 | bytes 1179648 | tf_op jit(solution)/shard_map/first_absorption/pallas_call | solution.py:302
  11.3 9.0 %collective-permute-start.2 = (bf16[1,192,768]{2,1,0:T(8,128)(2,1)S(1)}, bf16[1,192,768]{2,1,0:T(8,128)(2,1)S(1)}, u32[]{:S(2)}, u32[]{:S(2)}) collective-permute-start(bf16[1,192,768]{2,1,0:T(8,128)(2,1)S(1)} %first_absorption.1._after), channel_id=1, source_target_pairs={{0,8},{8,0},{16,24},{24,16},{32,40},{40,32},{48,56},{56,48},{64,72... | collective-permute-start | bytes 884744 | tf_op jit(solution)/shard_map/ppermute | solution.py:25
  20.3 3.7 %whole_first_absorption.1._after = bf16[1,192,768]{2,1,0:T(8,128)(2,1)S(1)} custom-call(s32[2,1,1,194]{3,2,1,0:T(1,128)S(1)} %collective-permute-done.from_left_ref, bf16[1,192,768]{2,1,0:T(8,128)(2,1)S(1)} %first_absorption.1._after, s32[1,1,2]{2,1,0:T(1,128)} %bitcast.2, s32[2,1,1,4,4]{4,3,2,1,0:T(4,128)} %leg_in.7, s32[2,1,1,2]{3,2,1,0:T(1,128)} %rank_in.7, ...), custom_call_target="tpu_custom_call" | custom-call | flops 471859200 | bytes 1179648 | tf_op jit(solution)/shard_map/whole_first_absorption/pallas_call | solution.py:307
  24.0 1.9 %collective-permute-start.1 = (bf16[1,192,768]{2,1,0:T(8,128)(2,1)S(1)}, bf16[1,192,768]{2,1,0:T(8,128)(2,1)S(1)}, u32[]{:S(2)}, u32[]{:S(2)}) collective-permute-start(bf16[1,192,768]{2,1,0:T(8,128)(2,1)S(1)} %whole_first_absorption.1._after), channel_id=1, source_target_pairs={{0,8},{8,0},{16,24},{24,16},{32,40},{40,32},{48,56},{56,48},{64,72... | collective-permute-start | bytes 884744 | tf_op jit(solution)/shard_map/ppermute | solution.py:25
  25.9 1.8 %prepare_second.3 = (bf16[768,192]{1,0:T(8,128)(2,1)S(1)}, bf16[256,256]{1,0:T(8,128)(2,1)S(1)}, bf16[1024,192]{1,0:T(8,128)(2,1)S(1)}) custom-call(bf16[1,192,768]{2,1,0:T(8,128)(2,1)S(1)} %whole_first_absorption.1._after, s32[1,1,2]{2,1,0:T(1,128)} %bitcast.3, s32[2,1,1,4,4]{4,3,2,1,0:T(4,128)} %leg_in.7, s32[2,1,1,2]{3,2,1,0:T(1,128)} %rank_in.7, ...), custom_call_target="tpu_custom_call" | custom-call | flops 471859200 | bytes 1179648 | tf_op jit(solution)/shard_map/prepare_second/pallas_call | solution.py:315
  27.7 1.8 %prepare_second.2 = (bf16[768,192]{1,0:T(8,128)(2,1)S(1)}, bf16[256,256]{1,0:T(8,128)(2,1)S(1)}, bf16[1024,192]{1,0:T(8,128)(2,1)S(1)}) custom-call(bf16[1,192,768]{2,1,0:T(8,128)(2,1)S(1)} %whole_first_absorption.1._after, s32[1,1,2]{2,1,0:T(1,128)} %bitcast.4, s32[2,1,1,4,4]{4,3,2,1,0:T(4,128)} %leg_in.7, s32[2,1,1,2]{3,2,1,0:T(1,128)} %rank_in.7, ...), custom_call_target="tpu_custom_call" | custom-call | flops 471859200 | bytes 1179648 | tf_op jit(solution)/shard_map/prepare_second/pallas_call | solution.py:315
  29.6 5.8 %collective-permute-done.2.received_ref = bf16[1,192,768]{2,1,0:T(8,128)(2,1)S(1)} collective-permute-done((bf16[1,192,768]{2,1,0:T(8,128)(2,1)S(1)}, bf16[1,192,768]{2,1,0:T(8,128)(2,1)S(1)}, u32[]{:S(2)}, u32[]{:S(2)}) %collective-permute-start.2) | collective-permute-done | bytes 294944 | tf_op jit(solution)/shard_map/ppermute | solution.py:25
  35.3 2.7 %second_absorption.2.rest_0_ = bf16[2,1,1,192,768]{4,3,2,1,0:T(8,128)(2,1)} custom-call(s32[2,1,1,194]{3,2,1,0:T(1,128)S(1)} %collective-permute-done.from_left_ref, bf16[1,192,768]{2,1,0:T(8,128)(2,1)S(1)} %collective-permute-done.2.received_ref, bf16[768,192]{1,0:T(8,128)(2,1)S(1)} %get-tuple-element.26.stack_ref, ...), custom_call_target="tpu_custom_call" | custom-call | flops 471859200 | bytes 1179648 | tf_op jit(solution)/shard_map/second_absorption/pallas_call | solution.py:324
  38.0 11.6 %collective-permute-done.1.received_ref = bf16[1,192,768]{2,1,0:T(8,128)(2,1)S(1)} collective-permute-done((bf16[1,192,768]{2,1,0:T(8,128)(2,1)S(1)}, bf16[1,192,768]{2,1,0:T(8,128)(2,1)S(1)}, u32[]{:S(2)}, u32[]{:S(2)}) %collective-permute-start.1) | collective-permute-done | bytes 294944 | tf_op jit(solution)/shard_map/ppermute | solution.py:25
  49.6 2.7 %second_absorption.3 = bf16[2,1,1,192,768]{4,3,2,1,0:T(8,128)(2,1)} custom-call(s32[2,1,1,194]{3,2,1,0:T(1,128)S(1)} %collective-permute-done.from_left_ref, bf16[1,192,768]{2,1,0:T(8,128)(2,1)S(1)} %collective-permute-done.1.received_ref, bf16[768,192]{1,0:T(8,128)(2,1)S(1)} %get-tuple-element.23.stack_ref, ...), custom_call_target="tpu_custom_call", output_to_operand_aliasing={{}: (5, {})} | custom-call | flops 471859200 | bytes 1179648 | tf_op jit(solution)/shard_map/second_absorption/pallas_call | solution.py:324
Async XLA Ops:
  0.8 8.6 %collective-permute-start = (s32[2,1,1,194]{3,2,1,0:T(1,128)S(1)}, s32[2,1,1,194]{3,2,1,0:T(1,128)S(1)}, u32[]{:S(2)}, u32[]{:S(2)}) collective-permute-start(s32[2,1,1,194]{3,2,1,0:T(1,128)S(1)} %pad_add_fusion), channel_id=1, source_target_pairs={{0,1},{1,2},{2,3},{3,4},{4,5},{5,6},{6,7},{7,0},{8,9},{9,10},{10,1... | collective-permute-start | bytes 4664 | tf_op jit(solution)/shard_map/ppermute | solution.py:19
  11.3 24.1 %collective-permute-start.2 = (bf16[1,192,768]{2,1,0:T(8,128)(2,1)S(1)}, bf16[1,192,768]{2,1,0:T(8,128)(2,1)S(1)}, u32[]{:S(2)}, u32[]{:S(2)}) collective-permute-start(bf16[1,192,768]{2,1,0:T(8,128)(2,1)S(1)} %first_absorption.1._after), channel_id=1, source_target_pairs={{0,8},{8,0},{16,24},{24,16},{32,40},{40,32},{48,56},{56,48},{64,72... | collective-permute-start | bytes 884744 | tf_op jit(solution)/shard_map/ppermute | solution.py:25
  24.0 25.6 %collective-permute-start.1 = (bf16[1,192,768]{2,1,0:T(8,128)(2,1)S(1)}, bf16[1,192,768]{2,1,0:T(8,128)(2,1)S(1)}, u32[]{:S(2)}, u32[]{:S(2)}) collective-permute-start(bf16[1,192,768]{2,1,0:T(8,128)(2,1)S(1)} %whole_first_absorption.1._after), channel_id=1, source_target_pairs={{0,8},{8,0},{16,24},{24,16},{32,40},{40,32},{48,56},{56,48},{64,72... | collective-permute-start | bytes 884744 | tf_op jit(solution)/shard_map/ppermute | solution.py:25

commit v2 on v1

v2 whole, which is shorter than its diff:
```python
import functools

import jax
import jax.numpy as jnp
from jax import lax
from jax.experimental import pallas as pl
from jax.experimental.pallas import tpu as pltpu
from jax.sharding import PartitionSpec as P

eps = 1e-06
VMEM_BYTES = 32 * 1024 * 1024
GROUP = 16
LANES = 128


def passed_along(value, axis, steps):
    count = lax.axis_size(axis)
    pairs = [(source, (source + steps) % count) for source in range(count)]
    return lax.ppermute(value, axis, pairs)


def swapped(value, axis, distance):
    mask = 2**distance
    pairs = [(source, source ^ mask) for source in range(lax.axis_size(axis))]
    return lax.ppermute(value, axis, pairs)


def pick(index, values):
    out = jnp.zeros_like(index)
    for j, value in enumerate(values):
        out = jnp.where(index == j, value, out)
    return out


def expand_block(s, legs, natural, site_ref, spin_ref, leg_ref, by_left_ref, by_right_ref, kron_ref):
    squared = legs * legs
    spin = spin_ref[0, 0, s]
    leg = [[leg_ref[s, 0, 0, j, t] for t in range(legs)] for j in range(4)]
    for l in range(legs):
        for e in range(legs):
            tile = jnp.where(spin == 1, site_ref[s, 0, 0, 1, l, e], site_ref[s, 0, 0, 0, l, e])
            tile = tile.astype(jnp.float32)
            by_left_ref[l * legs : (l + 1) * legs, e * legs : (e + 1) * legs] = tile
            by_right_ref[e * legs : (e + 1) * legs, l * legs : (l + 1) * legs] = tile
    turned = jnp.transpose(by_left_ref[...])[:squared, :squared]
    entries = jnp.where(natural, turned, by_right_ref[:squared, :squared])
    row = lax.broadcasted_iota(jnp.int32, (squared, squared), 0)
    col = lax.broadcasted_iota(jnp.int32, (squared, squared), 1)
    right, outer, left, inner = row // legs, row % legs, col // legs, col % legs
    up, down = jnp.where(natural, inner, outer), jnp.where(natural, outer, inner)
    balance = spin + pick(left, leg[0]) + pick(up, leg[2]) - pick(right, leg[1]) - pick(down, leg[3])
    entries = jnp.where(balance == 0, entries, 0.0).astype(jnp.bfloat16)
    size = squared * GROUP
    tall = lax.broadcasted_iota(jnp.int32, (size, squared), 0) // GROUP
    tall = (tall == lax.broadcasted_iota(jnp.int32, (size, squared), 1)).astype(jnp.bfloat16)
    wide = lax.broadcasted_iota(jnp.int32, (squared, size), 1) // GROUP
    wide = (wide == lax.broadcasted_iota(jnp.int32, (squared, size), 0)).astype(jnp.bfloat16)
    spread = jnp.dot(tall, entries, preferred_element_type=jnp.float32).astype(jnp.bfloat16)
    spread = jnp.dot(spread, wide, preferred_element_type=jnp.float32)
    row = lax.broadcasted_iota(jnp.int32, (size, size), 0)
    col = lax.broadcasted_iota(jnp.int32, (size, size), 1)
    kron_ref[...] = jnp.where(row % GROUP == col % GROUP, spread, 0.0).astype(jnp.bfloat16)


def stack_left(legs, width, rank, left_ref, stack_ref):
    for l in range(legs):
        part = left_ref[:, l * width : (l + 1) * width]
        if rank is not None:
            kept = lax.broadcasted_iota(jnp.int32, (width, 1), 0) < rank
            part = jnp.where(kept, part, jnp.zeros_like(part))
        stack_ref[l * width : (l + 1) * width, :] = part


def parts_of(width):
    return [(first, min(LANES, width - first)) for first in range(0, width, LANES)]


def turn_right(legs, width, rank, right_ref, turned_ref):
    kept = lax.broadcasted_iota(jnp.int32, (width, width), 1) < rank
    for e in range(legs):
        turned = jnp.transpose(right_ref[:, e * width : (e + 1) * width])
        turned = jnp.where(kept, turned, jnp.zeros_like(turned))
        for p, (first, length) in enumerate(parts_of(width)):
            at = (p * legs + e) * LANES
            turned_ref[at : at + length, :] = turned[first : first + length, :]
            if length < LANES:
                turned_ref[at + length : at + LANES, :] = jnp.zeros((LANES - length, width), jnp.bfloat16)


def combine(legs, width, given_ref, stack_ref, kron_ref, proj_ref, comb_ref, comb_at):
    for l in range(legs):
        proj = jnp.dot(stack_ref[l * width : (l + 1) * width, :], given_ref[...], preferred_element_type=jnp.float32)
        proj_ref[l * width : (l + 1) * width, :] = proj.astype(jnp.bfloat16)
    pair = 2 * GROUP

    def piece(l, i, k):
        return proj_ref[l * width + k : l * width + k + GROUP, i * LANES : (i + 1) * LANES]

    for q in range(0, width, pair):
        part = jnp.concatenate(
            [
                jnp.concatenate([piece(l, i, q), piece(l, i, q + GROUP)], axis=1)
                for l in range(legs)
                for i in range(legs)
            ],
            axis=0,
        )
        comb = jnp.dot(kron_ref[...], part, preferred_element_type=jnp.float32).astype(jnp.bfloat16)
        for e in range(legs):
            for o in range(legs):
                place = (e * legs + o) * GROUP
                for h in range(2):
                    row = o * width + q + h * GROUP
                    comb_ref[row : row + GROUP, comb_at + e * LANES : comb_at + (e + 1) * LANES] = (
                        comb[place : place + GROUP, h * LANES : (h + 1) * LANES]
                    )


def space_given(legs, width, given, spaced_refs):
    for spaced_ref, (first, length) in zip(spaced_refs, parts_of(width)):
        for i in range(legs):
            spaced_ref[:, i * LANES : i * LANES + length] = given[:, i * width + first : i * width + first + length]
            if length < LANES:
                spaced_ref[:, i * LANES + length : (i + 1) * LANES] = jnp.zeros((width, LANES - length), jnp.bfloat16)


def space_part(legs, width, p, received, spaced_ref):
    length = parts_of(width)[p][1]
    for i in range(legs):
        spaced_ref[:, i * LANES : i * LANES + length] = received[:, i * length : (i + 1) * length]
        if length < LANES:
            spaced_ref[:, i * LANES + length : (i + 1) * LANES] = jnp.zeros((width, LANES - length), jnp.bfloat16)


def absorb(legs, width, spaced_refs, stack_ref, kron_ref, turned_ref, proj_ref, comb_ref):
    for p, spaced_ref in enumerate(spaced_refs):
        combine(legs, width, spaced_ref, stack_ref, kron_ref, proj_ref, comb_ref, p * legs * LANES)
    return jnp.dot(comb_ref[...], turned_ref[...], preferred_element_type=jnp.float32)


def prepare(
    states, step, legs, width, rank_left,
    spin_in, leg_in, rank_in, site_in, left_in, right_in, ready_refs,
    spin_ref, leg_ref, rank_ref, site_ref, left_ref, right_ref, by_left_ref, by_right_ref, sems,
):
    small = [
        pltpu.make_async_copy(source, target, sems.at[j])
        for j, (source, target) in enumerate(
            [(spin_in, spin_ref), (leg_in, leg_ref), (rank_in, rank_ref), (site_in, site_ref)]
        )
    ]
    large = [
        pltpu.make_async_copy(source.at[s, 0, 0, step], target.at[s], sems.at[4 + 2 * s + j])
        for s in states
        for j, (source, target) in enumerate([(right_in, right_ref), (left_in, left_ref)])
    ]
    for copy in small + large:
        copy.start()
    for copy in small:
        copy.wait()
    natural = is_top_first() if step == 0 else jnp.logical_not(is_top_first())
    for n, s in enumerate(states):
        stack_ref, kron_ref, turned_ref = ready_refs[3 * n : 3 * n + 3]
        expand_block(s, legs, natural, site_ref, spin_ref, leg_ref, by_left_ref, by_right_ref, kron_ref)
        large[2 * n].wait()
        turn_right(legs, width, rank_ref[s, 0, 0, step], right_ref.at[s], turned_ref)
        large[2 * n + 1].wait()
        stack_left(legs, width, None if rank_left is None else rank_left(s), left_ref.at[s], stack_ref)


def rank_of(s, step, width, from_left_ref):
    return from_left_ref[s, 0, :, width + step : width + step + 1]


def is_top_first():
    return lax.rem(lax.axis_index("row"), 2) == 0


def prepare_first_kernel(states, legs, width, *rest):
    spin_in, leg_in, rank_in, site_in, charge_in, given_in, left_in, right_in = rest[:8]
    given_ref, charge_ref, incoming_ref, *rest = rest[8:]
    ready_refs, scratch, more = rest[: 3 * len(states)], rest[3 * len(states) : -1], rest[-1]
    copies = [
        pltpu.make_async_copy(given_in.at[:, 0, 0], given_ref, more.at[0]),
        pltpu.make_async_copy(charge_in, charge_ref, more.at[1]),
    ]
    for copy in copies:
        copy.start()
    prepare(
        states, 0, legs, width, None,
        spin_in, leg_in, rank_in, site_in, left_in, right_in, ready_refs, *scratch,
    )
    leg_ref = scratch[1]
    for s in states:
        for i in range(legs):
            incoming = jnp.where(is_top_first(), leg_ref[s, 0, 0, 2, i], leg_ref[s, 0, 0, 3, i])
            incoming_ref[s, i : i + 1, :] = jnp.full((1, LANES), incoming, jnp.int32)
    for copy in copies:
        copy.wait()


def prepare_second_kernel(states, legs, width, from_left_ref, _after, *rest):
    prepare(
        states, 1, legs, width, lambda s: rank_of(s, 1, width, from_left_ref),
        *rest[:6], rest[6 : 6 + 3 * len(states)], *rest[6 + 3 * len(states) :],
    )


def first_kernel(states, legs, width, from_left_ref, given_ref, charge_ref, incoming_ref, *rest):
    count = len(parts_of(width))
    ready_refs, half_refs = rest[: 3 * len(states)], rest[-2 - count - len(states) : -2 - count]
    spaced_refs, (proj_ref, comb_ref) = rest[-2 - count : -2], rest[-2:]
    for n, s in enumerate(states):
        stack_ref, kron_ref, turned_ref = ready_refs[3 * n : 3 * n + 3]
        half_ref = half_refs[n]
        row_charge = from_left_ref[s, 0, :, :width].astype(jnp.float32)
        left_charge = jnp.transpose(jnp.broadcast_to(row_charge, (LANES, width)))[:, :1]
        right_charge = charge_ref[s, 0].astype(jnp.float32)
        wanted = [right_charge - incoming_ref[s, i : i + 1, :1].astype(jnp.float32) for i in range(legs)]
        given = given_ref[s]
        given = jnp.where(left_charge == jnp.concatenate(wanted, axis=1), given, jnp.zeros_like(given))
        space_given(legs, width, given, spaced_refs)
        result = absorb(legs, width, spaced_refs, stack_ref, kron_ref, turned_ref, proj_ref, comb_ref)
        kept = lax.broadcasted_iota(jnp.int32, (width, 1), 0) < rank_of(s, 0, width, from_left_ref)
        base = 0
        for first, length in parts_of(width):
            for o in range(legs):
                part = jnp.where(kept, result[o * width : (o + 1) * width, first : first + length], 0.0)
                half_ref[:, base + o * length : base + (o + 1) * length] = part.astype(jnp.bfloat16)
            base += legs * length


def second_kernel(states, each, legs, width, *rest):
    count = len(parts_of(width))
    received_refs, rest = rest[: len(states) if each else 1], rest[len(states) if each else 1 :]
    ready_refs = rest[: 3 * len(states)]
    out_ref, spaced_refs = rest[-6 - count], rest[-5 - count : -5]
    proj_ref, comb_ref, sum_ref, final_ref, sems = rest[-5:]
    copies = []
    for n, s in enumerate(states):
        stack_ref, kron_ref, turned_ref = ready_refs[3 * n : 3 * n + 3]
        received_ref = received_refs[n] if each else received_refs[0].at[n]
        base = 0
        for p, (_, length) in enumerate(parts_of(width)):
            space_part(legs, width, p, received_ref[:, base : base + legs * length], spaced_refs[p])
            base += legs * length
        for p, spaced_ref in enumerate(spaced_refs):
            combine(legs, width, spaced_ref, stack_ref, kron_ref, proj_ref, comb_ref, p * legs * LANES)
        squares = jnp.zeros((1, width), jnp.float32)
        for o in range(legs):
            rows = slice(o * width, (o + 1) * width)
            part = jnp.dot(comb_ref[rows, :], turned_ref[...], preferred_element_type=jnp.float32)
            sum_ref[rows, :] = part
            squares = squares + jnp.sum(part * part, axis=0, keepdims=True)
        mean = jnp.sum(squares, axis=1, keepdims=True) * (1.0 / (legs * width * width))
        scale = lax.rsqrt(mean + eps)
        for o in range(legs):
            part = sum_ref[o * width : (o + 1) * width, :] * scale
            final_ref[n, :, o * width : (o + 1) * width] = part.astype(jnp.bfloat16)
        copies.append(pltpu.make_async_copy(final_ref.at[n], out_ref.at[s, 0, 0], sems.at[n]))
        copies[-1].start()
    for copy in copies:
        copy.wait()


def local(
    boundary_in,
    site_tensors,
    spin_config,
    leg_charges,
    bond_charges,
    left_proj,
    right_proj,
    proj_ranks,
):
    states, width, legs = boundary_in.shape[0], boundary_in.shape[3], site_tensors.shape[4]
    every = list(range(states))
    squared, long = legs * legs, legs * width
    size = squared * GROUP
    count = len(parts_of(width))
    vmem = pl.BlockSpec(memory_space=pltpu.VMEM)
    hbm = pl.BlockSpec(memory_space=pltpu.HBM)
    bf16, i32 = jnp.bfloat16, jnp.int32

    edge = jnp.concatenate([bond_charges, proj_ranks], axis=3)
    from_left = passed_along(edge, "col", 1)

    ready_shapes = [((long, width), bf16), ((size, size), bf16), ((count * legs * LANES, width), bf16)]
    given_shapes = [((states, width, long), bf16), (bond_charges.shape, i32), ((states, 8, LANES), i32)]
    prepare_scratch = [
        pltpu.SMEM((1, 1, states), i32),
        pltpu.SMEM(leg_charges.shape, i32),
        pltpu.SMEM(proj_ranks.shape, i32),
        pltpu.VMEM(site_tensors.shape, bf16),
        pltpu.VMEM((states, width, long), bf16),
        pltpu.VMEM((states, width, long), bf16),
        pltpu.VMEM((LANES, LANES), jnp.float32),
        pltpu.VMEM((LANES, LANES), jnp.float32),
        pltpu.SemaphoreType.DMA((4 + 2 * states,)),
    ]
    absorb_scratch = [pltpu.VMEM((width, legs * LANES), bf16)] * count + [
        pltpu.VMEM((long, legs * LANES), bf16),
        pltpu.VMEM((long, count * legs * LANES), bf16),
    ]
    flops = 2 * (2 * width * long * long + long * long * GROUP)

    def call(kernel, name, out_shapes, in_specs, scratch, out_specs, **options):
        return pl.pallas_call(
            kernel,
            out_shape=[jax.ShapeDtypeStruct(*shape) for shape in out_shapes],
            in_specs=in_specs,
            out_specs=out_specs,
            scratch_shapes=scratch,
            compiler_params=pltpu.CompilerParams(vmem_limit_bytes=VMEM_BYTES),
            cost_estimate=pl.CostEstimate(flops=flops, bytes_accessed=8 * width * long, transcendentals=0),
            name=name,
            **options,
        )

    spins = jnp.transpose(spin_config, (1, 2, 0))
    spins, leg_charges, proj_ranks, site_tensors, bond_charges, boundary_in, left_proj, right_proj = (
        pltpu.with_memory_space_constraint(value, pltpu.HBM)
        for value in (spins, leg_charges, proj_ranks, site_tensors, bond_charges, boundary_in, left_proj, right_proj)
    )
    small = (spins, leg_charges, proj_ranks, site_tensors)
    bind = functools.partial
    given, charges, incoming, *ready = call(
        bind(prepare_first_kernel, every, legs, width), "prepare_first", given_shapes + ready_shapes * states,
        [hbm] * 8, prepare_scratch + [pltpu.SemaphoreType.DMA((2,))], [vmem] * (3 + 3 * states),
    )(*small, bond_charges, boundary_in, left_proj, right_proj)
    halves, last = [], None
    for group in [[s] for s in every]:
        more = [] if last is None else [last]
        halves.append(
            call(
                bind(first_kernel, group, legs, width), "first_absorption", [((width, long), bf16)] * len(group),
                [vmem] * (4 + 3 * len(group) + len(more)), absorb_scratch, [vmem] * len(group),
            )(from_left, given, charges, incoming, *ready[3 * group[0] : 3 * group[-1] + 3], *more)
        )
        last = halves[-1][-1]
    received = [swapped(half, "row", 0) for group in halves for half in group]
    ready = call(
        bind(prepare_second_kernel, every, legs, width), "prepare_second", ready_shapes * states,
        [vmem] * 2 + [hbm] * 6, prepare_scratch, [vmem] * (3 * states),
    )(from_left, last, *small, left_proj, right_proj)
    out = None
    for group in [[s] for s in every]:
        more = [] if out is None else [out]
        (out,) = call(
            bind(second_kernel, group, True, legs, width), "second_absorption", [(boundary_in.shape, bf16)],
            [vmem] * (4 * len(group)) + [hbm] * len(more),
            absorb_scratch
            + [
                pltpu.VMEM((long, width), jnp.float32),
                pltpu.VMEM((len(group), width, long), bf16),
                pltpu.SemaphoreType.DMA((len(group),)),
            ],
            [hbm], input_output_aliases={4 * len(group): 0} if more else {},
        )(*[received[s] for s in group], *ready[3 * group[0] : 3 * group[-1] + 3], *more)
    return out


def solution(mesh):
    placed = (
        P(None, "row", "col", None, None),
        P(None, "row", "col", None, None, None, None, None),
        P(None, "row", "col"),
        P(None, "row", "col", None, None),
        P(None, "row", "col", None),
        P(None, "row", "col", None, None, None),
        P(None, "row", "col", None, None, None),
        P(None, "row", "col", None),
    )
    return jax.shard_map(
        local,
        mesh=mesh,
        in_specs=placed,
        out_specs=P(None, "row", "col", None, None),
        check_vma=False,
    )
```

time: 52.5 us -> 47.8 us (0.910)
  the two profiles are of different devices: /device:TPU:36 before, /device:TPU:111 now
where the time goes in v2:
time: 47.8 us; the launch traced here: 47.6 us
  waiting for transfers between devices  16.4 us (34%)
  starting transfers between devices  15.3 us (32%)
  Pallas kernels  15 us (31%)
  other arithmetic  0.77 us (2%)
    ppermute x2, waiting for transfers between devices, swapped(): return lax.ppermute(value, axis, pairs)  16.4 us
    ppermute x2, starting transfers between devices, swapped(): return lax.ppermute(value, axis, pairs)  10.8 us
    pallas_call x2, Pallas kernels, local(): call(bind(second_kernel, group, True, legs, width), 'second_absorption',...  5.42 us
    ppermute x1, starting transfers between devices, passed_along(): return lax.ppermute(value, axis, pairs)  4.55 us
    pallas_call x2, Pallas kernels, local(): call(bind(first_kernel, group, legs, width), 'first_absorption', [((width...  4.18 us
    pallas_call x1, Pallas kernels, local(): call(bind(prepare_first_kernel, every, legs, width), 'prepare_first', giv...  2.79 us
    pallas_call x1, Pallas kernels, local(): call(bind(prepare_second_kernel, every, legs, width), 'prepare_second', r...  2.65 us
  transfers between devices with their start and end apart: 3, of which 2 were waited for; matrix products, arithmetic and copies ran while one was open for 0% of the time, Pallas kernels for 22%

profile of v2, /device:TPU:111, one launch (start us, length us, event | category | flops | bytes accessed | tf_op | source)
XLA Modules:
  0.0 47.6 jit_solution(5222606139506262014)
XLA Ops:
  0.0 0.8 %pad_add_fusion = s32[2,1,1,194]{3,2,1,0:T(1,128)S(1)} fusion(s32[2,1,1,2]{3,2,1,0:T(1,128)} %rest_2_.3, s32[2,1,1,192]{3,2,1,0:T(1,128)} %rest_4_.2), kind=kLoop, calls=%fused_computation | loop fusion | flops 388 | bytes 3104 | tf_op jit(solution)/shard_map/concatenate | solution.py:285
  0.8 4.6 %collective-permute-start = (s32[2,1,1,194]{3,2,1,0:T(1,128)S(1)}, s32[2,1,1,194]{3,2,1,0:T(1,128)S(1)}, u32[]{:S(2)}, u32[]{:S(2)}) collective-permute-start(s32[2,1,1,194]{3,2,1,0:T(1,128)S(1)} %pad_add_fusion), channel_id=1, source_target_pairs={{0,1},{1,2},{2,3},{3,4},{4,5},{5,6},{6,7},{7,0},{8,9},{9,10},{10,1... | collective-permute-start | bytes 4664 | tf_op jit(solution)/shard_map/ppermute | solution.py:19
  5.3 2.8 %prepare_first.1 = (bf16[2,192,768]{2,1,0:T(8,128)(2,1)S(1)}, s32[2,1,1,192]{3,2,1,0:T(1,128)S(1)}, s32[2,8,128]{2,1,0:T(8,128)S(1)}, bf16[768,192]{1,0:T(8,128)...) custom-call(s32[1,1,2]{2,1,0:T(1,128)} %bitcast.1, ...), custom_call_target="tpu_custom_call" | custom-call | flops 471859200 | bytes 1179648 | tf_op jit(solution)/shard_map/prepare_first/pallas_call | solution.py:327
  8.1 0.0 collective-permute-done.from_left_ref
  8.1 2.1 %first_absorption.2.rest_3_ = bf16[192,768]{1,0:T(8,128)(2,1)S(1)} custom-call(s32[2,1,1,194]{3,2,1,0:T(1,128)S(1)} %collective-permute-done.from_left_ref, bf16[2,192,768]{2,1,0:T(8,128)(2,1)S(1)} %get-tuple-element.20.given_ref, s32[2,1,1,192]{3,2,1,0:T(1,128)S(1)} %get-tuple-element.21.charge_ref, s32[2,8,128]{2,1,0:T(8,128)S(1)} %get-tuple-element.22.incoming_ref, ...), custom_call_target="tpu_custom_call" | custom-call | flops 471859200 | bytes 1179648 | tf_op jit(solution)/shard_map/first_absorption/pallas_call | solution.py:335
  10.2 8.8 %collective-permute-start.2 = (bf16[192,768]{1,0:T(8,128)(2,1)S(1)}, bf16[192,768]{1,0:T(8,128)(2,1)S(1)}, u32[]{:S(2)}, u32[]{:S(2)}) collective-permute-start(bf16[192,768]{1,0:T(8,128)(2,1)S(1)} %first_absorption.2.rest_3_), channel_id=1, source_target_pairs={{0,8},{8,0},{16,24},{24,16},{32,40},{40,32},{48,56},{56,48},{64,72... | collective-permute-start | bytes 884744 | tf_op jit(solution)/shard_map/ppermute | solution.py:25
  19.1 2.1 %first_absorption.3._after = bf16[192,768]{1,0:T(8,128)(2,1)S(1)} custom-call(s32[2,1,1,194]{3,2,1,0:T(1,128)S(1)} %collective-permute-done.from_left_ref, bf16[2,192,768]{2,1,0:T(8,128)(2,1)S(1)} %get-tuple-element.20.given_ref, s32[2,1,1,192]{3,2,1,0:T(1,128)S(1)} %get-tuple-element.21.charge_ref, s32[2,8,128]{2,1,0:T(8,128)S(1)} %get-tuple-element.22.incoming_ref, ...), custom_call_target="tpu_custom_call" | custom-call | flops 471859200 | bytes 1179648 | tf_op jit(solution)/shard_map/first_absorption/pallas_call | solution.py:335
  21.2 1.9 %collective-permute-start.1 = (bf16[192,768]{1,0:T(8,128)(2,1)S(1)}, bf16[192,768]{1,0:T(8,128)(2,1)S(1)}, u32[]{:S(2)}, u32[]{:S(2)}) collective-permute-start(bf16[192,768]{1,0:T(8,128)(2,1)S(1)} %first_absorption.3._after), channel_id=1, source_target_pairs={{0,8},{8,0},{16,24},{24,16},{32,40},{40,32},{48,56},{56,48},{64,72... | collective-permute-start | bytes 884744 | tf_op jit(solution)/shard_map/ppermute | solution.py:25
  23.1 2.6 %prepare_second.1 = (bf16[768,192]{1,0:T(8,128)(2,1)S(1)}, bf16[256,256]{1,0:T(8,128)(2,1)S(1)}, bf16[1024,192]{1,0:T(8,128)(2,1)S(1)}, bf16[768,192]{1,0:T(8,12...) custom-call(s32[2,1,1,194]{3,2,1,0:T(1,128)S(1)} %collective-permute-done.from_left_ref, ...), custom_call_target="tpu_custom_call" | custom-call | flops 471859200 | bytes 1179648 | tf_op jit(solution)/shard_map/prepare_second/pallas_call | solution.py:342
  25.8 9.7 %collective-permute-done.2.rest_0_ = bf16[192,768]{1,0:T(8,128)(2,1)S(1)} collective-permute-done((bf16[192,768]{1,0:T(8,128)(2,1)S(1)}, bf16[192,768]{1,0:T(8,128)(2,1)S(1)}, u32[]{:S(2)}, u32[]{:S(2)}) %collective-permute-start.2) | collective-permute-done | bytes 294944 | tf_op jit(solution)/shard_map/ppermute | solution.py:25
  35.4 2.7 %second_absorption.2.rest_4_ = bf16[2,1,1,192,768]{4,3,2,1,0:T(8,128)(2,1)} custom-call(bf16[192,768]{1,0:T(8,128)(2,1)S(1)} %collective-permute-done.2.rest_0_, bf16[768,192]{1,0:T(8,128)(2,1)S(1)} %get-tuple-element.32.rest_1_, bf16[256,256]{1,0:T(8,128)(2,1)S(1)} %get-tuple-element.33.rest_2_, bf16[1024,192]{1,0:T(8,128)(2,1)S(1)} %get-tuple-element.34.rest_3_), custom_call_target="tpu_custom_call" | custom-call | flops 471859200 | bytes 1179648 | tf_op jit(solution)/shard_map/second_absorption/pallas_call | solution.py:349
  38.2 6.7 %collective-permute-done.1.rest_0_ = bf16[192,768]{1,0:T(8,128)(2,1)S(1)} collective-permute-done((bf16[192,768]{1,0:T(8,128)(2,1)S(1)}, bf16[192,768]{1,0:T(8,128)(2,1)S(1)}, u32[]{:S(2)}, u32[]{:S(2)}) %collective-permute-start.1) | collective-permute-done | bytes 294944 | tf_op jit(solution)/shard_map/ppermute | solution.py:25
  44.8 2.7 %second_absorption.3 = bf16[2,1,1,192,768]{4,3,2,1,0:T(8,128)(2,1)} custom-call(bf16[192,768]{1,0:T(8,128)(2,1)S(1)} %collective-permute-done.1.rest_0_, bf16[768,192]{1,0:T(8,128)(2,1)S(1)} %get-tuple-element.29.rest_1_, bf16[256,256]{1,0:T(8,128)(2,1)S(1)} %get-tuple-element.30.rest_2_, ...), custom_call_target="tpu_custom_call", output_to_operand_aliasing={{}: (4, {})} | custom-call | flops 471859200 | bytes 1179648 | tf_op jit(solution)/shard_map/second_absorption/pallas_call | solution.py:349
Async XLA Ops:
  0.8 7.4 %collective-permute-start = (s32[2,1,1,194]{3,2,1,0:T(1,128)S(1)}, s32[2,1,1,194]{3,2,1,0:T(1,128)S(1)}, u32[]{:S(2)}, u32[]{:S(2)}) collective-permute-start(s32[2,1,1,194]{3,2,1,0:T(1,128)S(1)} %pad_add_fusion), channel_id=1, source_target_pairs={{0,1},{1,2},{2,3},{3,4},{4,5},{5,6},{6,7},{7,0},{8,9},{9,10},{10,1... | collective-permute-start | bytes 4664 | tf_op jit(solution)/shard_map/ppermute | solution.py:19
  10.2 25.2 %collective-permute-start.2 = (bf16[192,768]{1,0:T(8,128)(2,1)S(1)}, bf16[192,768]{1,0:T(8,128)(2,1)S(1)}, u32[]{:S(2)}, u32[]{:S(2)}) collective-permute-start(bf16[192,768]{1,0:T(8,128)(2,1)S(1)} %first_absorption.2.rest_3_), channel_id=1, source_target_pairs={{0,8},{8,0},{16,24},{24,16},{32,40},{40,32},{48,56},{56,48},{64,72... | collective-permute-start | bytes 884744 | tf_op jit(solution)/shard_map/ppermute | solution.py:25
  21.2 23.7 %collective-permute-start.1 = (bf16[192,768]{1,0:T(8,128)(2,1)S(1)}, bf16[192,768]{1,0:T(8,128)(2,1)S(1)}, u32[]{:S(2)}, u32[]{:S(2)}) collective-permute-start(bf16[192,768]{1,0:T(8,128)(2,1)S(1)} %first_absorption.3._after), channel_id=1, source_target_pairs={{0,8},{8,0},{16,24},{24,16},{32,40},{40,32},{48,56},{56,48},{64,72... | collective-permute-start | bytes 884744 | tf_op jit(solution)/shard_map/ppermute | solution.py:25

commit v3 on v2

--- a/solution.py
+++ b/solution.py
@@ -80,62 +80,66 @@
     for e in range(legs):
         turned = jnp.transpose(right_ref[:, e * width : (e + 1) * width])
         turned = jnp.where(kept, turned, jnp.zeros_like(turned))
-        for p, (first, length) in enumerate(parts_of(width)):
-            at = (p * legs + e) * LANES
+        for first, length in parts_of(width):
+            at = legs * first + e * length
             turned_ref[at : at + length, :] = turned[first : first + length, :]
-            if length < LANES:
-                turned_ref[at + length : at + LANES, :] = jnp.zeros((LANES - length, width), jnp.bfloat16)
-
-
-def combine(legs, width, given_ref, stack_ref, kron_ref, proj_ref, comb_ref, comb_at):
+
+
+def project(legs, width, given, stack_ref, proj_ref):
     for l in range(legs):
-        proj = jnp.dot(stack_ref[l * width : (l + 1) * width, :], given_ref[...], preferred_element_type=jnp.float32)
-        proj_ref[l * width : (l + 1) * width, :] = proj.astype(jnp.bfloat16)
-    pair = 2 * GROUP
-
-    def piece(l, i, k):
-        return proj_ref[l * width + k : l * width + k + GROUP, i * LANES : (i + 1) * LANES]
-
-    for q in range(0, width, pair):
+        rows = slice(l * width, (l + 1) * width)
+        proj = jnp.dot(stack_ref[rows, :], given, preferred_element_type=jnp.float32)
+        proj_ref[rows, :] = proj.astype(jnp.bfloat16)
+
+
+def combine(legs, width, length, kron_ref, proj_ref, comb_ref):
+    side = 2 * LANES // length
+    for q in range(0, width, side * GROUP):
+        places = [q + h * GROUP for h in range(side)]
         part = jnp.concatenate(
             [
-                jnp.concatenate([piece(l, i, q), piece(l, i, q + GROUP)], axis=1)
+                jnp.concatenate(
+                    [
+                        proj_ref[l * width + k : l * width + k + GROUP, i * length : (i + 1) * length]
+                        for k in places
+                    ],
+                    axis=1,
+                )
                 for l in range(legs)
                 for i in range(legs)
             ],
             axis=0,
         )
         comb = jnp.dot(kron_ref[...], part, preferred_element_type=jnp.float32).astype(jnp.bfloat16)
-        for e in range(legs):
-            for o in range(legs):
-                place = (e * legs + o) * GROUP
-                for h in range(2):
-                    row = o * width + q + h * GROUP
-                    comb_ref[row : row + GROUP, comb_at + e * LANES : comb_at + (e + 1) * LANES] = (
-                        comb[place : place + GROUP, h * LANES : (h + 1) * LANES]
-                    )
-
-
-def space_given(legs, width, given, spaced_refs):
-    for spaced_ref, (first, length) in zip(spaced_refs, parts_of(width)):
-        for i in range(legs):
-            spaced_ref[:, i * LANES : i * LANES + length] = given[:, i * width + first : i * width + first + length]
-            if length < LANES:
-                spaced_ref[:, i * LANES + length : (i + 1) * LANES] = jnp.zeros((width, LANES - length), jnp.bfloat16)
-
-
-def space_part(legs, width, p, received, spaced_ref):
-    length = parts_of(width)[p][1]
-    for i in range(legs):
-        spaced_ref[:, i * LANES : i * LANES + length] = received[:, i * length : (i + 1) * length]
-        if length < LANES:
-            spaced_ref[:, i * LANES + length : (i + 1) * LANES] = jnp.zeros((width, LANES - length), jnp.bfloat16)
-
-
-def absorb(legs, width, spaced_refs, stack_ref, kron_ref, turned_ref, proj_ref, comb_ref):
-    for p, spaced_ref in enumerate(spaced_refs):
-        combine(legs, width, spaced_ref, stack_ref, kron_ref, proj_ref, comb_ref, p * legs * LANES)
-    return jnp.dot(comb_ref[...], turned_ref[...], preferred_element_type=jnp.float32)
+        for o in range(legs):
+            for h, k in enumerate(places):
+                comb_ref[o * width + k : o * width + k + GROUP, :] = jnp.concatenate(
+                    [
+                        comb[(e * legs + o) * GROUP : (e * legs + o + 1) * GROUP, h * length : (h + 1) * length]
+                        for e in range(legs)
+                    ],
+                    axis=1,
+                )
+
+
+def absorb(legs, width, givens, stack_ref, kron_ref, turned_ref, proj_refs, comb_refs):
+    parts = parts_of(width)
+    for given, proj_ref in zip(givens, proj_refs):
+        project(legs, width, given, stack_ref, proj_ref)
+    for (_, length), proj_ref, comb_ref in zip(parts, proj_refs, comb_refs):
+        combine(legs, width, length, kron_ref, proj_ref, comb_ref)
+    results = []
+    for o in range(legs):
+        result = None
+        for (first, length), comb_ref in zip(parts, comb_refs):
+            term = jnp.dot(
+                comb_ref[o * width : (o + 1) * width, :],
+                turned_ref[legs * first : legs * (first + length), :],
+                preferred_element_type=jnp.float32,
+            )
+            result = term if result is None else result + term
+        results.append(result)
+    return results
 
 
 def prepare(
@@ -156,15 +160,13 @@
     ]
     for copy in small + large:
         copy.start()
-    for copy in small:
+    for copy in small + large:
         copy.wait()
     natural = is_top_first() if step == 0 else jnp.logical_not(is_top_first())
     for n, s in enumerate(states):
         stack_ref, kron_ref, turned_ref = ready_refs[3 * n : 3 * n + 3]
         expand_block(s, legs, natural, site_ref, spin_ref, leg_ref, by_left_ref, by_right_ref, kron_ref)
-        large[2 * n].wait()
         turn_right(legs, width, rank_ref[s, 0, 0, step], right_ref.at[s], turned_ref)
-        large[2 * n + 1].wait()
         stack_left(legs, width, None if rank_left is None else rank_left(s), left_ref.at[s], stack_ref)
 
 
@@ -207,56 +209,49 @@
 
 
 def first_kernel(states, legs, width, from_left_ref, given_ref, charge_ref, incoming_ref, *rest):
-    count = len(parts_of(width))
-    ready_refs, half_refs = rest[: 3 * len(states)], rest[-2 - count - len(states) : -2 - count]
-    spaced_refs, (proj_ref, comb_ref) = rest[-2 - count : -2], rest[-2:]
+    parts = parts_of(width)
+    count = len(parts)
+    ready_refs, half_refs = rest[: 3 * len(states)], rest[-3 * count - len(states) : -3 * count]
+    given_refs, proj_refs, comb_refs = rest[-3 * count : -2 * count], rest[-2 * count : -count], rest[-count:]
     for n, s in enumerate(states):
-        stack_ref, kron_ref, turned_ref = ready_refs[3 * n : 3 * n + 3]
-        half_ref = half_refs[n]
         row_charge = from_left_ref[s, 0, :, :width].astype(jnp.float32)
         left_charge = jnp.transpose(jnp.broadcast_to(row_charge, (LANES, width)))[:, :1]
         right_charge = charge_ref[s, 0].astype(jnp.float32)
         wanted = [right_charge - incoming_ref[s, i : i + 1, :1].astype(jnp.float32) for i in range(legs)]
         given = given_ref[s]
         given = jnp.where(left_charge == jnp.concatenate(wanted, axis=1), given, jnp.zeros_like(given))
-        space_given(legs, width, given, spaced_refs)
-        result = absorb(legs, width, spaced_refs, stack_ref, kron_ref, turned_ref, proj_ref, comb_ref)
+        for part_ref, (first, length) in zip(given_refs, parts):
+            for i in range(legs):
+                at = i * width + first
+                part_ref[:, i * length : (i + 1) * length] = given[:, at : at + length]
+        givens = [part_ref[...] for part_ref in given_refs]
+        results = absorb(legs, width, givens, *ready_refs[3 * n : 3 * n + 3], proj_refs, comb_refs)
         kept = lax.broadcasted_iota(jnp.int32, (width, 1), 0) < rank_of(s, 0, width, from_left_ref)
-        base = 0
-        for first, length in parts_of(width):
-            for o in range(legs):
-                part = jnp.where(kept, result[o * width : (o + 1) * width, first : first + length], 0.0)
-                half_ref[:, base + o * length : base + (o + 1) * length] = part.astype(jnp.bfloat16)
-            base += legs * length
-
-
-def second_kernel(states, each, legs, width, *rest):
-    count = len(parts_of(width))
-    received_refs, rest = rest[: len(states) if each else 1], rest[len(states) if each else 1 :]
-    ready_refs = rest[: 3 * len(states)]
-    out_ref, spaced_refs = rest[-6 - count], rest[-5 - count : -5]
-    proj_ref, comb_ref, sum_ref, final_ref, sems = rest[-5:]
+        for first, length in parts:
+            for o, result in enumerate(results):
+                part = jnp.where(kept, result[:, first : first + length], 0.0)
+                at = legs * first + o * length
+                half_refs[n][:, at : at + length] = part.astype(jnp.bfloat16)
+
+
+def second_kernel(states, legs, width, *rest):
+    parts = parts_of(width)
+    count = len(parts)
+    received_refs, ready_refs = rest[: len(states)], rest[len(states) : 4 * len(states)]
+    proj_refs, comb_refs = rest[-3 - 2 * count : -3 - count], rest[-3 - count : -3]
+    out_ref, (sum_ref, final_ref, sems) = rest[-4 - 2 * count], rest[-3:]
     copies = []
     for n, s in enumerate(states):
-        stack_ref, kron_ref, turned_ref = ready_refs[3 * n : 3 * n + 3]
-        received_ref = received_refs[n] if each else received_refs[0].at[n]
-        base = 0
-        for p, (_, length) in enumerate(parts_of(width)):
-            space_part(legs, width, p, received_ref[:, base : base + legs * length], spaced_refs[p])
-            base += legs * length
-        for p, spaced_ref in enumerate(spaced_refs):
-            combine(legs, width, spaced_ref, stack_ref, kron_ref, proj_ref, comb_ref, p * legs * LANES)
+        givens = [received_refs[n][:, legs * first : legs * (first + length)] for first, length in parts]
+        results = absorb(legs, width, givens, *ready_refs[3 * n : 3 * n + 3], proj_refs, comb_refs)
         squares = jnp.zeros((1, width), jnp.float32)
-        for o in range(legs):
-            rows = slice(o * width, (o + 1) * width)
-            part = jnp.dot(comb_ref[rows, :], turned_ref[...], preferred_element_type=jnp.float32)
-            sum_ref[rows, :] = part
-            squares = squares + jnp.sum(part * part, axis=0, keepdims=True)
+        for o, result in enumerate(results):
+            sum_ref[o] = result
+            squares = squares + jnp.sum(result * result, axis=0, keepdims=True)
         mean = jnp.sum(squares, axis=1, keepdims=True) * (1.0 / (legs * width * width))
         scale = lax.rsqrt(mean + eps)
         for o in range(legs):
-            part = sum_ref[o * width : (o + 1) * width, :] * scale
-            final_ref[n, :, o * width : (o + 1) * width] = part.astype(jnp.bfloat16)
+            final_ref[n, :, o * width : (o + 1) * width] = (sum_ref[o] * scale).astype(jnp.bfloat16)
         copies.append(pltpu.make_async_copy(final_ref.at[n], out_ref.at[s, 0, 0], sems.at[n]))
         copies[-1].start()
     for copy in copies:
@@ -277,7 +272,6 @@
     every = list(range(states))
     squared, long = legs * legs, legs * width
     size = squared * GROUP
-    count = len(parts_of(width))
     vmem = pl.BlockSpec(memory_space=pltpu.VMEM)
     hbm = pl.BlockSpec(memory_space=pltpu.HBM)
     bf16, i32 = jnp.bfloat16, jnp.int32
@@ -285,7 +279,7 @@
     edge = jnp.concatenate([bond_charges, proj_ranks], axis=3)
     from_left = passed_along(edge, "col", 1)
 
-    ready_shapes = [((long, width), bf16), ((size, size), bf16), ((count * legs * LANES, width), bf16)]
+    ready_shapes = [((long, width), bf16), ((size, size), bf16), ((long, width), bf16)]
     given_shapes = [((states, width, long), bf16), (bond_charges.shape, i32), ((states, 8, LANES), i32)]
     prepare_scratch = [
         pltpu.SMEM((1, 1, states), i32),
@@ -298,10 +292,8 @@
         pltpu.VMEM((LANES, LANES), jnp.float32),
         pltpu.SemaphoreType.DMA((4 + 2 * states,)),
     ]
-    absorb_scratch = [pltpu.VMEM((width, legs * LANES), bf16)] * count + [
-        pltpu.VMEM((long, legs * LANES), bf16),
-        pltpu.VMEM((long, count * legs * LANES), bf16),
-    ]
+    given_scratch = [pltpu.VMEM((width, legs * length), bf16) for _, length in parts_of(width)]
+    absorb_scratch = [pltpu.VMEM((long, legs * length), bf16) for _, length in parts_of(width)] * 2
     flops = 2 * (2 * width * long * long + long * long * GROUP)
 
     def call(kernel, name, out_shapes, in_specs, scratch, out_specs, **options):
@@ -334,7 +326,7 @@
         halves.append(
             call(
                 bind(first_kernel, group, legs, width), "first_absorption", [((width, long), bf16)] * len(group),
-                [vmem] * (4 + 3 * len(group) + len(more)), absorb_scratch, [vmem] * len(group),
+                [vmem] * (4 + 3 * len(group) + len(more)), given_scratch + absorb_scratch, [vmem] * len(group),
             )(from_left, given, charges, incoming, *ready[3 * group[0] : 3 * group[-1] + 3], *more)
         )
         last = halves[-1][-1]
@@ -347,11 +339,11 @@
     for group in [[s] for s in every]:
         more = [] if out is None else [out]
         (out,) = call(
-            bind(second_kernel, group, True, legs, width), "second_absorption", [(boundary_in.shape, bf16)],
+            bind(second_kernel, group, legs, width), "second_absorption", [(boundary_in.shape, bf16)],
             [vmem] * (4 * len(group)) + [hbm] * len(more),
             absorb_scratch
             + [
-                pltpu.VMEM((long, width), jnp.float32),
+                pltpu.VMEM((legs, width, width), jnp.float32),
                 pltpu.VMEM((len(group), width, long), bf16),
                 pltpu.SemaphoreType.DMA((len(group),)),
             ],

time: 47.8 us -> 46.9 us (0.981)
  the two profiles are of different devices: /device:TPU:111 before, /device:TPU:113 now
where the time goes in v3:
time: 46.9 us; the launch traced here: 46.6 us
  waiting for transfers between devices  18.1 us (39%)
  starting transfers between devices  15.3 us (33%)
  Pallas kernels  12.4 us (26%)
  other arithmetic  0.77 us (2%)
    ppermute x2, waiting for transfers between devices, swapped(): return lax.ppermute(value, axis, pairs)  18.1 us
    ppermute x2, starting transfers between devices, swapped(): return lax.ppermute(value, axis, pairs)  10.8 us
    ppermute x1, starting transfers between devices, passed_along(): return lax.ppermute(value, axis, pairs)  4.55 us
    pallas_call x2, Pallas kernels, local(): call(bind(second_kernel, group, legs, width), 'second_absorption', [(boun...  4.47 us
    pallas_call x2, Pallas kernels, local(): call(bind(first_kernel, group, legs, width), 'first_absorption', [((width...  3.24 us
    pallas_call x1, Pallas kernels, local(): call(bind(prepare_first_kernel, every, legs, width), 'prepare_first', giv...  2.36 us
    pallas_call x1, Pallas kernels, local(): call(bind(prepare_second_kernel, every, legs, width), 'prepare_second', r...  2.35 us
  transfers between devices with their start and end apart: 3, of which 2 were waited for; matrix products, arithmetic and copies ran while one was open for 0% of the time, Pallas kernels for 18%

profile of v3, /device:TPU:113, one launch (start us, length us, event | category | flops | bytes accessed | tf_op | source)
XLA Modules:
  0.0 46.6 jit_solution(15212688887155530998)
XLA Ops:
  0.0 0.8 %pad_add_fusion = s32[2,1,1,194]{3,2,1,0:T(1,128)S(1)} fusion(s32[2,1,1,2]{3,2,1,0:T(1,128)} %rest_2_.3, s32[2,1,1,192]{3,2,1,0:T(1,128)} %rest_4_.2), kind=kLoop, calls=%fused_computation | loop fusion | flops 388 | bytes 3104 | tf_op jit(solution)/shard_map/concatenate | solution.py:279
  0.8 4.6 %collective-permute-start = (s32[2,1,1,194]{3,2,1,0:T(1,128)S(1)}, s32[2,1,1,194]{3,2,1,0:T(1,128)S(1)}, u32[]{:S(2)}, u32[]{:S(2)}) collective-permute-start(s32[2,1,1,194]{3,2,1,0:T(1,128)S(1)} %pad_add_fusion), channel_id=1, source_target_pairs={{0,1},{1,2},{2,3},{3,4},{4,5},{5,6},{6,7},{7,0},{8,9},{9,10},{10,1... | collective-permute-start | bytes 4664 | tf_op jit(solution)/shard_map/ppermute | solution.py:19
  5.3 2.4 %prepare_first.1 = (bf16[2,192,768]{2,1,0:T(8,128)(2,1)S(1)}, s32[2,1,1,192]{3,2,1,0:T(1,128)S(1)}, s32[2,8,128]{2,1,0:T(8,128)S(1)}, bf16[768,192]{1,0:T(8,128)...) custom-call(s32[1,1,2]{2,1,0:T(1,128)} %bitcast.1, ...), custom_call_target="tpu_custom_call" | custom-call | flops 471859200 | bytes 1179648 | tf_op jit(solution)/shard_map/prepare_first/pallas_call | solution.py:319
  7.7 0.0 collective-permute-done.from_left_ref
  7.7 1.6 %first_absorption.2.rest_3_ = bf16[192,768]{1,0:T(8,128)(2,1)S(1)} custom-call(s32[2,1,1,194]{3,2,1,0:T(1,128)S(1)} %collective-permute-done.from_left_ref, bf16[2,192,768]{2,1,0:T(8,128)(2,1)S(1)} %get-tuple-element.20.given_ref, s32[2,1,1,192]{3,2,1,0:T(1,128)S(1)} %get-tuple-element.21.charge_ref, s32[2,8,128]{2,1,0:T(8,128)S(1)} %get-tuple-element.22.incoming_ref, ...), custom_call_target="tpu_custom_call" | custom-call | flops 471859200 | bytes 1179648 | tf_op jit(solution)/shard_map/first_absorption/pallas_call | solution.py:327
  9.3 8.8 %collective-permute-start.2 = (bf16[192,768]{1,0:T(8,128)(2,1)S(1)}, bf16[192,768]{1,0:T(8,128)(2,1)S(1)}, u32[]{:S(2)}, u32[]{:S(2)}) collective-permute-start(bf16[192,768]{1,0:T(8,128)(2,1)S(1)} %first_absorption.2.rest_3_), channel_id=1, source_target_pairs={{0,8},{8,0},{16,24},{24,16},{32,40},{40,32},{48,56},{56,48},{64,72... | collective-permute-start | bytes 884744 | tf_op jit(solution)/shard_map/ppermute | solution.py:25
  18.2 1.6 %first_absorption.3._after = bf16[192,768]{1,0:T(8,128)(2,1)S(1)} custom-call(s32[2,1,1,194]{3,2,1,0:T(1,128)S(1)} %collective-permute-done.from_left_ref, bf16[2,192,768]{2,1,0:T(8,128)(2,1)S(1)} %get-tuple-element.20.given_ref, s32[2,1,1,192]{3,2,1,0:T(1,128)S(1)} %get-tuple-element.21.charge_ref, s32[2,8,128]{2,1,0:T(8,128)S(1)} %get-tuple-element.22.incoming_ref, ...), custom_call_target="tpu_custom_call" | custom-call | flops 471859200 | bytes 1179648 | tf_op jit(solution)/shard_map/first_absorption/pallas_call | solution.py:327
  19.8 1.9 %collective-permute-start.1 = (bf16[192,768]{1,0:T(8,128)(2,1)S(1)}, bf16[192,768]{1,0:T(8,128)(2,1)S(1)}, u32[]{:S(2)}, u32[]{:S(2)}) collective-permute-start(bf16[192,768]{1,0:T(8,128)(2,1)S(1)} %first_absorption.3._after), channel_id=1, source_target_pairs={{0,8},{8,0},{16,24},{24,16},{32,40},{40,32},{48,56},{56,48},{64,72... | collective-permute-start | bytes 884744 | tf_op jit(solution)/shard_map/ppermute | solution.py:25
  21.7 2.4 %prepare_second.1 = (bf16[768,192]{1,0:T(8,128)(2,1)S(1)}, bf16[256,256]{1,0:T(8,128)(2,1)S(1)}, bf16[768,192]{1,0:T(8,128)(2,1)S(1)}, bf16[768,192]{1,0:T(8,128...) custom-call(s32[2,1,1,194]{3,2,1,0:T(1,128)S(1)} %collective-permute-done.from_left_ref, ...), custom_call_target="tpu_custom_call" | custom-call | flops 471859200 | bytes 1179648 | tf_op jit(solution)/shard_map/prepare_second/pallas_call | solution.py:334
  24.1 11.2 %collective-permute-done.2.rest_0_ = bf16[192,768]{1,0:T(8,128)(2,1)S(1)} collective-permute-done((bf16[192,768]{1,0:T(8,128)(2,1)S(1)}, bf16[192,768]{1,0:T(8,128)(2,1)S(1)}, u32[]{:S(2)}, u32[]{:S(2)}) %collective-permute-start.2) | collective-permute-done | bytes 294944 | tf_op jit(solution)/shard_map/ppermute | solution.py:25
  35.3 2.2 %second_absorption.2.rest_4_ = bf16[2,1,1,192,768]{4,3,2,1,0:T(8,128)(2,1)} custom-call(bf16[192,768]{1,0:T(8,128)(2,1)S(1)} %collective-permute-done.2.rest_0_, bf16[768,192]{1,0:T(8,128)(2,1)S(1)} %get-tuple-element.32.rest_1_, bf16[256,256]{1,0:T(8,128)(2,1)S(1)} %get-tuple-element.33.rest_2_, bf16[768,192]{1,0:T(8,128)(2,1)S(1)} %get-tuple-element.34.rest_3_), custom_call_target="tpu_custom_call" | custom-call | flops 471859200 | bytes 1179648 | tf_op jit(solution)/shard_map/second_absorption/pallas_call | solution.py:341
  37.5 6.9 %collective-permute-done.1.rest_0_ = bf16[192,768]{1,0:T(8,128)(2,1)S(1)} collective-permute-done((bf16[192,768]{1,0:T(8,128)(2,1)S(1)}, bf16[192,768]{1,0:T(8,128)(2,1)S(1)}, u32[]{:S(2)}, u32[]{:S(2)}) %collective-permute-start.1) | collective-permute-done | bytes 294944 | tf_op jit(solution)/shard_map/ppermute | solution.py:25
  44.4 2.2 %second_absorption.3 = bf16[2,1,1,192,768]{4,3,2,1,0:T(8,128)(2,1)} custom-call(bf16[192,768]{1,0:T(8,128)(2,1)S(1)} %collective-permute-done.1.rest_0_, bf16[768,192]{1,0:T(8,128)(2,1)S(1)} %get-tuple-element.29.rest_1_, bf16[256,256]{1,0:T(8,128)(2,1)S(1)} %get-tuple-element.30.rest_2_, ...), custom_call_target="tpu_custom_call", output_to_operand_aliasing={{}: (4, {})} | custom-call | flops 471859200 | bytes 1179648 | tf_op jit(solution)/shard_map/second_absorption/pallas_call | solution.py:341
Async XLA Ops:
  0.8 6.9 %collective-permute-start = (s32[2,1,1,194]{3,2,1,0:T(1,128)S(1)}, s32[2,1,1,194]{3,2,1,0:T(1,128)S(1)}, u32[]{:S(2)}, u32[]{:S(2)}) collective-permute-start(s32[2,1,1,194]{3,2,1,0:T(1,128)S(1)} %pad_add_fusion), channel_id=1, source_target_pairs={{0,1},{1,2},{2,3},{3,4},{4,5},{5,6},{6,7},{7,0},{8,9},{9,10},{10,1... | collective-permute-start | bytes 4664 | tf_op jit(solution)/shard_map/ppermute | solution.py:19
  9.3 25.9 %collective-permute-start.2 = (bf16[192,768]{1,0:T(8,128)(2,1)S(1)}, bf16[192,768]{1,0:T(8,128)(2,1)S(1)}, u32[]{:S(2)}, u32[]{:S(2)}) collective-permute-start(bf16[192,768]{1,0:T(8,128)(2,1)S(1)} %first_absorption.2.rest_3_), channel_id=1, source_target_pairs={{0,8},{8,0},{16,24},{24,16},{32,40},{40,32},{48,56},{56,48},{64,72... | collective-permute-start | bytes 884744 | tf_op jit(solution)/shard_map/ppermute | solution.py:25
  19.8 24.6 %collective-permute-start.1 = (bf16[192,768]{1,0:T(8,128)(2,1)S(1)}, bf16[192,768]{1,0:T(8,128)(2,1)S(1)}, u32[]{:S(2)}, u32[]{:S(2)}) collective-permute-start(bf16[192,768]{1,0:T(8,128)(2,1)S(1)} %first_absorption.3._after), channel_id=1, source_target_pairs={{0,8},{8,0},{16,24},{24,16},{32,40},{40,32},{48,56},{56,48},{64,72... | collective-permute-start | bytes 884744 | tf_op jit(solution)/shard_map/ppermute | solution.py:25

commit v4 on v3

--- a/solution.py
+++ b/solution.py
@@ -143,26 +143,26 @@
 
 
 def prepare(
-    states, step, legs, width, rank_left,
+    states, step, legs, width, natural, rank_left, fetch_small,
     spin_in, leg_in, rank_in, site_in, left_in, right_in, ready_refs,
     spin_ref, leg_ref, rank_ref, site_ref, left_ref, right_ref, by_left_ref, by_right_ref, sems,
 ):
-    small = [
-        pltpu.make_async_copy(source, target, sems.at[j])
-        for j, (source, target) in enumerate(
-            [(spin_in, spin_ref), (leg_in, leg_ref), (rank_in, rank_ref), (site_in, site_ref)]
-        )
-    ]
-    large = [
+    copies = [
         pltpu.make_async_copy(source.at[s, 0, 0, step], target.at[s], sems.at[4 + 2 * s + j])
         for s in states
         for j, (source, target) in enumerate([(right_in, right_ref), (left_in, left_ref)])
     ]
-    for copy in small + large:
+    if fetch_small:
+        copies += [
+            pltpu.make_async_copy(source, target, sems.at[j])
+            for j, (source, target) in enumerate(
+                [(spin_in, spin_ref), (leg_in, leg_ref), (rank_in, rank_ref), (site_in, site_ref)]
+            )
+        ]
+    for copy in copies:
         copy.start()
-    for copy in small + large:
+    for copy in copies:
         copy.wait()
-    natural = is_top_first() if step == 0 else jnp.logical_not(is_top_first())
     for n, s in enumerate(states):
         stack_ref, kron_ref, turned_ref = ready_refs[3 * n : 3 * n + 3]
         expand_block(s, legs, natural, site_ref, spin_ref, leg_ref, by_left_ref, by_right_ref, kron_ref)
@@ -182,56 +182,100 @@
     spin_in, leg_in, rank_in, site_in, charge_in, given_in, left_in, right_in = rest[:8]
     given_ref, charge_ref, incoming_ref, *rest = rest[8:]
     ready_refs, scratch, more = rest[: 3 * len(states)], rest[3 * len(states) : -1], rest[-1]
+    sources = (spin_in, leg_in, rank_in, site_in, left_in, right_in)
+    top_first = is_top_first()
     copies = [
-        pltpu.make_async_copy(given_in.at[:, 0, 0], given_ref, more.at[0]),
+        pltpu.make_async_copy(given_in.at[0, 0, 0], given_ref.at[0], more.at[0]),
         pltpu.make_async_copy(charge_in, charge_ref, more.at[1]),
     ]
     for copy in copies:
         copy.start()
-    prepare(
-        states, 0, legs, width, None,
-        spin_in, leg_in, rank_in, site_in, left_in, right_in, ready_refs, *scratch,
-    )
+    prepare(states[:1], 0, legs, width, top_first, None, True, *sources, ready_refs[:3], *scratch)
     leg_ref = scratch[1]
     for s in states:
         for i in range(legs):
-            incoming = jnp.where(is_top_first(), leg_ref[s, 0, 0, 2, i], leg_ref[s, 0, 0, 3, i])
+            incoming = jnp.where(top_first, leg_ref[s, 0, 0, 2, i], leg_ref[s, 0, 0, 3, i])
             incoming_ref[s, i : i + 1, :] = jnp.full((1, LANES), incoming, jnp.int32)
     for copy in copies:
         copy.wait()
 
+    @pl.when(top_first)
+    def _():
+        fetches = [pltpu.make_async_copy(given_in.at[s, 0, 0], given_ref.at[s], more.at[s + 1]) for s in states[1:]]
+        for fetch in fetches:
+            fetch.start()
+        prepare(states[1:], 0, legs, width, top_first, None, False, *sources, ready_refs[3:], *scratch)
+        for fetch in fetches:
+            fetch.wait()
+
 
 def prepare_second_kernel(states, legs, width, from_left_ref, _after, *rest):
     prepare(
-        states, 1, legs, width, lambda s: rank_of(s, 1, width, from_left_ref),
+        states, 1, legs, width, jnp.logical_not(is_top_first()), lambda s: rank_of(s, 1, width, from_left_ref), True,
         *rest[:6], rest[6 : 6 + 3 * len(states)], *rest[6 + 3 * len(states) :],
     )
 
 
-def first_kernel(states, legs, width, from_left_ref, given_ref, charge_ref, incoming_ref, *rest):
+def absorb_first(
+    s, legs, width, from_left_ref, given_ref, charge_ref, incoming_ref, ready_refs, half_ref, scratch
+):
     parts = parts_of(width)
     count = len(parts)
-    ready_refs, half_refs = rest[: 3 * len(states)], rest[-3 * count - len(states) : -3 * count]
-    given_refs, proj_refs, comb_refs = rest[-3 * count : -2 * count], rest[-2 * count : -count], rest[-count:]
-    for n, s in enumerate(states):
-        row_charge = from_left_ref[s, 0, :, :width].astype(jnp.float32)
-        left_charge = jnp.transpose(jnp.broadcast_to(row_charge, (LANES, width)))[:, :1]
-        right_charge = charge_ref[s, 0].astype(jnp.float32)
-        wanted = [right_charge - incoming_ref[s, i : i + 1, :1].astype(jnp.float32) for i in range(legs)]
-        given = given_ref[s]
-        given = jnp.where(left_charge == jnp.concatenate(wanted, axis=1), given, jnp.zeros_like(given))
-        for part_ref, (first, length) in zip(given_refs, parts):
-            for i in range(legs):
-                at = i * width + first
-                part_ref[:, i * length : (i + 1) * length] = given[:, at : at + length]
-        givens = [part_ref[...] for part_ref in given_refs]
-        results = absorb(legs, width, givens, *ready_refs[3 * n : 3 * n + 3], proj_refs, comb_refs)
-        kept = lax.broadcasted_iota(jnp.int32, (width, 1), 0) < rank_of(s, 0, width, from_left_ref)
-        for first, length in parts:
-            for o, result in enumerate(results):
-                part = jnp.where(kept, result[:, first : first + length], 0.0)
-                at = legs * first + o * length
-                half_refs[n][:, at : at + length] = part.astype(jnp.bfloat16)
+    given_refs, proj_refs, comb_refs = scratch[:count], scratch[count : 2 * count], scratch[2 * count :]
+    row_charge = from_left_ref[s, 0, :, :width].astype(jnp.float32)
+    left_charge = jnp.transpose(jnp.broadcast_to(row_charge, (LANES, width)))[:, :1]
+    right_charge = charge_ref[s, 0].astype(jnp.float32)
+    wanted = [right_charge - incoming_ref[s, i : i + 1, :1].astype(jnp.float32) for i in range(legs)]
+    given = given_ref[s]
+    given = jnp.where(left_charge == jnp.concatenate(wanted, axis=1), given, jnp.zeros_like(given))
+    for part_ref, (first, length) in zip(given_refs, parts):
+        for i in range(legs):
+            at = i * width + first
+            part_ref[:, i * length : (i + 1) * length] = given[:, at : at + length]
+    givens = [part_ref[...] for part_ref in given_refs]
+    results = absorb(legs, width, givens, *ready_refs, proj_refs, comb_refs)
+    kept = lax.broadcasted_iota(jnp.int32, (width, 1), 0) < rank_of(s, 0, width, from_left_ref)
+    for first, length in parts:
+        for o, result in enumerate(results):
+            part = jnp.where(kept, result[:, first : first + length], 0.0)
+            at = legs * first + o * length
+            half_ref[:, at : at + length] = part.astype(jnp.bfloat16)
+
+
+def first_kernel(states, legs, width, from_left_ref, given_ref, charge_ref, incoming_ref, *rest):
+    count = len(states)
+    ready_refs, half_refs, scratch = rest[: 3 * count], rest[3 * count : 4 * count], rest[4 * count :]
+    edges = (from_left_ref, given_ref, charge_ref, incoming_ref)
+    absorb_first(0, legs, width, *edges, ready_refs[:3], half_refs[0], scratch)
+
+    @pl.when(is_top_first())
+    def _():
+        for s in states[1:]:
+            absorb_first(s, legs, width, *edges, ready_refs[3 * s : 3 * s + 3], half_refs[s], scratch)
+
+
+def rest_kernel(s, legs, width, from_left_ref, charge_ref, incoming_ref, half_in_ref, _after, *rest):
+    spin_in, leg_in, rank_in, site_in, given_in, left_in, right_in, half_ref, given_ref = rest[:9]
+    ready_refs, sem, rest = rest[9:12], rest[12], rest[13:]
+    scratch, more = rest[: 3 * len(parts_of(width))], rest[3 * len(parts_of(width)) :]
+    top_first = is_top_first()
+
+    @pl.when(top_first)
+    def _():
+        half_ref[...] = half_in_ref[...]
+
+    @pl.when(jnp.logical_not(top_first))
+    def _():
+        fetch = pltpu.make_async_copy(given_in.at[s, 0, 0], given_ref.at[s], sem)
+        fetch.start()
+        prepare(
+            [s], 0, legs, width, top_first, None, True,
+            spin_in, leg_in, rank_in, site_in, left_in, right_in, ready_refs, *more,
+        )
+        fetch.wait()
+        absorb_first(
+            s, legs, width, from_left_ref, given_ref, charge_ref, incoming_ref, ready_refs, half_ref, scratch
+        )
 
 
 def second_kernel(states, legs, width, *rest):
@@ -318,19 +362,21 @@
     bind = functools.partial
     given, charges, incoming, *ready = call(
         bind(prepare_first_kernel, every, legs, width), "prepare_first", given_shapes + ready_shapes * states,
-        [hbm] * 8, prepare_scratch + [pltpu.SemaphoreType.DMA((2,))], [vmem] * (3 + 3 * states),
+        [hbm] * 8, prepare_scratch + [pltpu.SemaphoreType.DMA((1 + states,))], [vmem] * (3 + 3 * states),
     )(*small, bond_charges, boundary_in, left_proj, right_proj)
-    halves, last = [], None
-    for group in [[s] for s in every]:
-        more = [] if last is None else [last]
-        halves.append(
-            call(
-                bind(first_kernel, group, legs, width), "first_absorption", [((width, long), bf16)] * len(group),
-                [vmem] * (4 + 3 * len(group) + len(more)), given_scratch + absorb_scratch, [vmem] * len(group),
-            )(from_left, given, charges, incoming, *ready[3 * group[0] : 3 * group[-1] + 3], *more)
-        )
-        last = halves[-1][-1]
-    received = [swapped(half, "row", 0) for group in halves for half in group]
+    halves = list(call(
+        bind(first_kernel, every, legs, width), "first_absorption", [((width, long), bf16)] * states,
+        [vmem] * (4 + 3 * states), given_scratch + absorb_scratch, [vmem] * states,
+    )(from_left, given, charges, incoming, *ready))
+    for s in every[1:]:
+        halves[s : s + 1] = call(
+            bind(rest_kernel, s, legs, width), "first_absorption_rest", [((width, long), bf16)],
+            [vmem] * 5 + [hbm] * 7,
+            [pltpu.VMEM(*shape) for shape in given_shapes[:1] + ready_shapes]
+            + [pltpu.SemaphoreType.DMA] + given_scratch + absorb_scratch + prepare_scratch, [vmem],
+        )(from_left, charges, incoming, halves[s], halves[s - 1], *small, boundary_in, left_proj, right_proj)
+    last = halves[-1]
+    received = [swapped(half, "row", 0) for half in halves]
     ready = call(
         bind(prepare_second_kernel, every, legs, width), "prepare_second", ready_shapes * states,
         [vmem] * 2 + [hbm] * 6, prepare_scratch, [vmem] * (3 * states),

time: 46.9 us -> 46.5 us (level)
  the two profiles are of different devices: /device:TPU:113 before, /device:TPU:193 now
where the time goes in v4:
time: 46.5 us; the launch traced here: 46.3 us
  starting transfers between devices  17.8 us (38%)
  waiting for transfers between devices  14.1 us (30%)
  Pallas kernels  13.5 us (29%)
  other arithmetic  0.77 us (2%)
    ppermute x2, waiting for transfers between devices, swapped(): return lax.ppermute(value, axis, pairs)  14.1 us
    ppermute x2, starting transfers between devices, swapped(): return lax.ppermute(value, axis, pairs)  12.4 us
    ppermute x1, starting transfers between devices, passed_along(): return lax.ppermute(value, axis, pairs)  5.39 us
    pallas_call x2, Pallas kernels, local(): call(bind(second_kernel, group, legs, width), 'second_absorption', [(boun...  4.48 us
    pallas_call x1, Pallas kernels, local(): call(bind(prepare_first_kernel, every, legs, width), 'prepare_first', giv...  3.36 us
    pallas_call x1, Pallas kernels, local(): call(bind(first_kernel, every, legs, width), 'first_absorption', [((width...  3.25 us
    pallas_call x1, Pallas kernels, local(): call(bind(prepare_second_kernel, every, legs, width), 'prepare_second', r...  2.34 us
  transfers between devices with their start and end apart: 3, of which 2 were waited for; matrix products, arithmetic and copies ran while one was open for 0% of the time, Pallas kernels for 17%

profile of v4, /device:TPU:193, one launch (start us, length us, event | category | flops | bytes accessed | tf_op | source)
XLA Modules:
  0.0 46.3 jit_solution(12543455228469038563)
XLA Ops:
  0.0 0.8 %pad_add_fusion = s32[2,1,1,194]{3,2,1,0:T(1,128)S(1)} fusion(s32[2,1,1,2]{3,2,1,0:T(1,128)} %rest_2_.5, s32[2,1,1,192]{3,2,1,0:T(1,128)} %rest_4_.3), kind=kLoop, calls=%fused_computation | loop fusion | flops 388 | bytes 3104 | tf_op jit(solution)/shard_map/concatenate | solution.py:323
  0.8 5.4 %collective-permute-start = (s32[2,1,1,194]{3,2,1,0:T(1,128)S(1)}, s32[2,1,1,194]{3,2,1,0:T(1,128)S(1)}, u32[]{:S(2)}, u32[]{:S(2)}) collective-permute-start(s32[2,1,1,194]{3,2,1,0:T(1,128)S(1)} %pad_add_fusion), channel_id=1, source_target_pairs={{0,1},{1,2},{2,3},{3,4},{4,5},{5,6},{6,7},{7,0},{8,9},{9,10},{10,1... | collective-permute-start | bytes 4664 | tf_op jit(solution)/shard_map/ppermute | solution.py:19
  6.2 3.4 %prepare_first.1 = (bf16[2,192,768]{2,1,0:T(8,128)(2,1)S(1)}, s32[2,1,1,192]{3,2,1,0:T(1,128)S(1)}, s32[2,8,128]{2,1,0:T(8,128)S(1)}, bf16[768,192]{1,0:T(8,128)...) custom-call(s32[1,1,2]{2,1,0:T(1,128)} %bitcast.1, ...), custom_call_target="tpu_custom_call" | custom-call | flops 471859200 | bytes 1179648 | tf_op jit(solution)/shard_map/prepare_first/pallas_call | solution.py:363
  9.5 0.0 collective-permute-done.from_left_ref
  9.5 3.2 %first_absorption.1 = (bf16[192,768]{1,0:T(8,128)(2,1)S(1)}, bf16[192,768]{1,0:T(8,128)(2,1)S(1)}) custom-call(s32[2,1,1,194]{3,2,1,0:T(1,128)S(1)} %collective-permute-done.from_left_ref, bf16[2,192,768]{2,1,0:T(8,128)(2,1)S(1)} %get-tuple-element.24.given_ref, s32[2,1,1,192]{3,2,1,0:T(1,128)S(1)} %get-tuple-element.22.charge_ref, ...), custom_call_target="tpu_custom_call" | custom-call | flops 471859200 | bytes 1179648 | tf_op jit(solution)/shard_map/first_absorption/pallas_call | solution.py:367
  12.8 2.0 %collective-permute-start.2 = (bf16[192,768]{1,0:T(8,128)(2,1)S(1)}, bf16[192,768]{1,0:T(8,128)(2,1)S(1)}, u32[]{:S(2)}, u32[]{:S(2)}) collective-permute-start(bf16[192,768]{1,0:T(8,128)(2,1)S(1)} %get-tuple-element.32._after), channel_id=1, source_target_pairs={{0,8},{8,0},{16,24},{24,16},{32,40},{40,32},{48,56},{56,48},{64,72... | collective-permute-start | bytes 884744 | tf_op jit(solution)/shard_map/ppermute | solution.py:25
  14.8 0.1 first_absorption_rest.1._after
  14.9 10.4 %collective-permute-start.1 = (bf16[192,768]{1,0:T(8,128)(2,1)S(1)}, bf16[192,768]{1,0:T(8,128)(2,1)S(1)}, u32[]{:S(2)}, u32[]{:S(2)}) collective-permute-start(bf16[192,768]{1,0:T(8,128)(2,1)S(1)} %first_absorption_rest.1._after), channel_id=1, source_target_pairs={{0,8},{8,0},{16,24},{24,16},{32,40},{40,32},{48,56},{56,48},{64,72... | collective-permute-start | bytes 884744 | tf_op jit(solution)/shard_map/ppermute | solution.py:25
  25.4 2.3 %prepare_second.1 = (bf16[768,192]{1,0:T(8,128)(2,1)S(1)}, bf16[256,256]{1,0:T(8,128)(2,1)S(1)}, bf16[768,192]{1,0:T(8,128)(2,1)S(1)}, bf16[768,192]{1,0:T(8,128...) custom-call(s32[2,1,1,194]{3,2,1,0:T(1,128)S(1)} %collective-permute-done.from_left_ref, ...), custom_call_target="tpu_custom_call" | custom-call | flops 471859200 | bytes 1179648 | tf_op jit(solution)/shard_map/prepare_second/pallas_call | solution.py:380
  27.7 11.7 %collective-permute-done.2.rest_0_ = bf16[192,768]{1,0:T(8,128)(2,1)S(1)} collective-permute-done((bf16[192,768]{1,0:T(8,128)(2,1)S(1)}, bf16[192,768]{1,0:T(8,128)(2,1)S(1)}, u32[]{:S(2)}, u32[]{:S(2)}) %collective-permute-start.2) | collective-permute-done | bytes 294944 | tf_op jit(solution)/shard_map/ppermute | solution.py:25
  39.4 2.2 %second_absorption.2.rest_4_ = bf16[2,1,1,192,768]{4,3,2,1,0:T(8,128)(2,1)} custom-call(bf16[192,768]{1,0:T(8,128)(2,1)S(1)} %collective-permute-done.2.rest_0_, bf16[768,192]{1,0:T(8,128)(2,1)S(1)} %get-tuple-element.36.rest_1_, bf16[256,256]{1,0:T(8,128)(2,1)S(1)} %get-tuple-element.37.rest_2_, bf16[768,192]{1,0:T(8,128)(2,1)S(1)} %get-tuple-element.38.rest_3_), custom_call_target="tpu_custom_call" | custom-call | flops 471859200 | bytes 1179648 | tf_op jit(solution)/shard_map/second_absorption/pallas_call | solution.py:387
  41.6 2.4 %collective-permute-done.1.rest_0_ = bf16[192,768]{1,0:T(8,128)(2,1)S(1)} collective-permute-done((bf16[192,768]{1,0:T(8,128)(2,1)S(1)}, bf16[192,768]{1,0:T(8,128)(2,1)S(1)}, u32[]{:S(2)}, u32[]{:S(2)}) %collective-permute-start.1) | collective-permute-done | bytes 294944 | tf_op jit(solution)/shard_map/ppermute | solution.py:25
  44.0 2.2 %second_absorption.3 = bf16[2,1,1,192,768]{4,3,2,1,0:T(8,128)(2,1)} custom-call(bf16[192,768]{1,0:T(8,128)(2,1)S(1)} %collective-permute-done.1.rest_0_, bf16[768,192]{1,0:T(8,128)(2,1)S(1)} %get-tuple-element.33.rest_1_, bf16[256,256]{1,0:T(8,128)(2,1)S(1)} %get-tuple-element.34.rest_2_, ...), custom_call_target="tpu_custom_call", output_to_operand_aliasing={{}: (4, {})} | custom-call | flops 471859200 | bytes 1179648 | tf_op jit(solution)/shard_map/second_absorption/pallas_call | solution.py:387
Async XLA Ops:
  0.8 8.8 %collective-permute-start = (s32[2,1,1,194]{3,2,1,0:T(1,128)S(1)}, s32[2,1,1,194]{3,2,1,0:T(1,128)S(1)}, u32[]{:S(2)}, u32[]{:S(2)}) collective-permute-start(s32[2,1,1,194]{3,2,1,0:T(1,128)S(1)} %pad_add_fusion), channel_id=1, source_target_pairs={{0,1},{1,2},{2,3},{3,4},{4,5},{5,6},{6,7},{7,0},{8,9},{9,10},{10,1... | collective-permute-start | bytes 4664 | tf_op jit(solution)/shard_map/ppermute | solution.py:19
  12.8 26.6 %collective-permute-start.2 = (bf16[192,768]{1,0:T(8,128)(2,1)S(1)}, bf16[192,768]{1,0:T(8,128)(2,1)S(1)}, u32[]{:S(2)}, u32[]{:S(2)}) collective-permute-start(bf16[192,768]{1,0:T(8,128)(2,1)S(1)} %get-tuple-element.32._after), channel_id=1, source_target_pairs={{0,8},{8,0},{16,24},{24,16},{32,40},{40,32},{48,56},{56,48},{64,72... | collective-permute-start | bytes 884744 | tf_op jit(solution)/shard_map/ppermute | solution.py:25
  14.9 29.1 %collective-permute-start.1 = (bf16[192,768]{1,0:T(8,128)(2,1)S(1)}, bf16[192,768]{1,0:T(8,128)(2,1)S(1)}, u32[]{:S(2)}, u32[]{:S(2)}) collective-permute-start(bf16[192,768]{1,0:T(8,128)(2,1)S(1)} %first_absorption_rest.1._after), channel_id=1, source_target_pairs={{0,8},{8,0},{16,24},{24,16},{32,40},{40,32},{48,56},{56,48},{64,72... | collective-permute-start | bytes 884744 | tf_op jit(solution)/shard_map/ppermute | solution.py:25

commit v5 on v4

--- a/solution.py
+++ b/solution.py
@@ -122,8 +122,8 @@
                 )
 
 
-def absorb(legs, width, givens, stack_ref, kron_ref, turned_ref, proj_refs, comb_refs):
-    parts = parts_of(width)
+def absorb(legs, width, givens, stack_ref, kron_ref, turned_ref, proj_refs, comb_refs, parts=None):
+    parts = parts or parts_of(width)
     for given, proj_ref in zip(givens, proj_refs):
         project(legs, width, given, stack_ref, proj_ref)
     for (_, length), proj_ref, comb_ref in zip(parts, proj_refs, comb_refs):
@@ -238,8 +238,11 @@
     for first, length in parts:
         for o, result in enumerate(results):
             part = jnp.where(kept, result[:, first : first + length], 0.0)
-            at = legs * first + o * length
-            half_ref[:, at : at + length] = part.astype(jnp.bfloat16)
+            if isinstance(half_ref, tuple):
+                target_ref, at = half_ref[parts.index((first, length))], o * length
+            else:
+                target_ref, at = half_ref, legs * first + o * length
+            target_ref[:, at : at + length] = part.astype(jnp.bfloat16)
 
 
 def first_kernel(states, legs, width, from_left_ref, given_ref, charge_ref, incoming_ref, *rest):
@@ -255,14 +258,17 @@
 
 
 def rest_kernel(s, legs, width, from_left_ref, charge_ref, incoming_ref, half_in_ref, _after, *rest):
-    spin_in, leg_in, rank_in, site_in, given_in, left_in, right_in, half_ref, given_ref = rest[:9]
-    ready_refs, sem, rest = rest[9:12], rest[12], rest[13:]
+    parts = parts_of(width)
+    spin_in, leg_in, rank_in, site_in, given_in, left_in, right_in = rest[:7]
+    half_refs, given_ref, rest = tuple(rest[7 : 7 + len(parts)]), rest[7 + len(parts)], rest[8 + len(parts) :]
+    ready_refs, sem, rest = rest[:3], rest[3], rest[4:]
     scratch, more = rest[: 3 * len(parts_of(width))], rest[3 * len(parts_of(width)) :]
     top_first = is_top_first()
 
     @pl.when(top_first)
     def _():
-        half_ref[...] = half_in_ref[...]
+        for half_ref, (first, length) in zip(half_refs, parts):
+            half_ref[...] = half_in_ref[:, legs * first : legs * (first + length)]
 
     @pl.when(jnp.logical_not(top_first))
     def _():
@@ -274,7 +280,7 @@
         )
         fetch.wait()
         absorb_first(
-            s, legs, width, from_left_ref, given_ref, charge_ref, incoming_ref, ready_refs, half_ref, scratch
+            s, legs, width, from_left_ref, given_ref, charge_ref, incoming_ref, ready_refs, half_refs, scratch
         )
 
 
@@ -302,6 +308,34 @@
         copy.wait()
 
 
+def second_part_kernel(p, legs, width, received_ref, *rest):
+    *rest, total_ref, proj_ref, comb_ref = rest
+    before = rest[4:]
+    results = absorb(
+        legs, width, [received_ref[...]], *rest[:3], [proj_ref], [comb_ref], parts_of(width)[p : p + 1]
+    )
+    for o, result in enumerate(results):
+        total_ref[o] = before[0][o] + result if before else result
+
+
+def second_last_kernel(s, p, legs, width, received_ref, stack_ref, kron_ref, turned_ref, total_ref, _out, *rest):
+    out_ref, proj_ref, comb_ref, sum_ref, final_ref, sem = rest
+    ready_refs = (stack_ref, kron_ref, turned_ref)
+    results = absorb(legs, width, [received_ref[...]], *ready_refs, [proj_ref], [comb_ref], parts_of(width)[p : p + 1])
+    squares = jnp.zeros((1, width), jnp.float32)
+    for o, result in enumerate(results):
+        result = total_ref[o] + result
+        sum_ref[o] = result
+        squares = squares + jnp.sum(result * result, axis=0, keepdims=True)
+    mean = jnp.sum(squares, axis=1, keepdims=True) * (1.0 / (legs * width * width))
+    scale = lax.rsqrt(mean + eps)
+    for o in range(legs):
+        final_ref[:, o * width : (o + 1) * width] = (sum_ref[o] * scale).astype(jnp.bfloat16)
+    copy = pltpu.make_async_copy(final_ref, out_ref.at[s, 0, 0], sem)
+    copy.start()
+    copy.wait()
+
+
 def local(
     boundary_in,
     site_tensors,
@@ -368,21 +402,24 @@
         bind(first_kernel, every, legs, width), "first_absorption", [((width, long), bf16)] * states,
         [vmem] * (4 + 3 * states), given_scratch + absorb_scratch, [vmem] * states,
     )(from_left, given, charges, incoming, *ready))
-    for s in every[1:]:
-        halves[s : s + 1] = call(
-            bind(rest_kernel, s, legs, width), "first_absorption_rest", [((width, long), bf16)],
-            [vmem] * 5 + [hbm] * 7,
-            [pltpu.VMEM(*shape) for shape in given_shapes[:1] + ready_shapes]
-            + [pltpu.SemaphoreType.DMA] + given_scratch + absorb_scratch + prepare_scratch, [vmem],
-        )(from_left, charges, incoming, halves[s], halves[s - 1], *small, boundary_in, left_proj, right_proj)
-    last = halves[-1]
-    received = [swapped(half, "row", 0) for half in halves]
+    s = states - 1
+    split = call(
+        bind(rest_kernel, s, legs, width), "first_absorption_rest",
+        [((width, legs * length), bf16) for _, length in parts_of(width)], [vmem] * 5 + [hbm] * 7,
+        [pltpu.VMEM(*shape) for shape in given_shapes[:1] + ready_shapes]
+        + [pltpu.SemaphoreType.DMA] + given_scratch + absorb_scratch + prepare_scratch, [vmem] * len(parts_of(width)),
+    )(from_left, charges, incoming, halves[s], halves[s - 1], *small, boundary_in, left_proj, right_proj)
+    last = split[0]
     ready = call(
         bind(prepare_second_kernel, every, legs, width), "prepare_second", ready_shapes * states,
         [vmem] * 2 + [hbm] * 6, prepare_scratch, [vmem] * (3 * states),
     )(from_left, last, *small, left_proj, right_proj)
+    *others, tail = split
+    tail, ready = lax.optimization_barrier((tail, ready))
+    received = [swapped(half, "row", 0) for half in halves[:-1]]
+    last_received = [swapped(part, "row", 0) for part in (*others, tail)]
     out = None
-    for group in [[s] for s in every]:
+    for group in [[s] for s in every[:-1]]:
         more = [] if out is None else [out]
         (out,) = call(
             bind(second_kernel, group, legs, width), "second_absorption", [(boundary_in.shape, bf16)],
@@ -395,6 +432,21 @@
             ],
             [hbm], input_output_aliases={4 * len(group): 0} if more else {},
         )(*[received[s] for s in group], *ready[3 * group[0] : 3 * group[-1] + 3], *more)
+    out = pltpu.with_memory_space_constraint(out, pltpu.HBM)
+    own, total = ready[-3:], []
+    for p, (_, length) in enumerate(parts_of(width)[:-1]):
+        total = call(
+            bind(second_part_kernel, p, legs, width), "second_absorption_part", [((legs, width, width), jnp.float32)],
+            [vmem] * 4 + [hbm] + [vmem] * len(total), [pltpu.VMEM((long, legs * length), bf16)] * 2, [vmem],
+        )(last_received[p], *own, out, *total)
+    length = parts_of(width)[-1][1]
+    (out,) = call(
+        bind(second_last_kernel, states - 1, len(parts_of(width)) - 1, legs, width), "second_absorption_last",
+        [(boundary_in.shape, bf16)], [vmem] * 5 + [hbm],
+        [pltpu.VMEM((long, legs * length), bf16)] * 2
+        + [pltpu.VMEM((legs, width, width), jnp.float32), pltpu.VMEM((width, long), bf16), pltpu.SemaphoreType.DMA],
+        [hbm], input_output_aliases={5: 0},
+    )(last_received[-1], *own, *total, out)
     return out
 
 

time: 46.5 us -> 46.1 us (level)
  waiting for transfers between devices: 14.1 us -> 11.2 us
  starting transfers between devices: 17.8 us -> 19.7 us
  Pallas kernels: 13.5 us -> 14.1 us
    ppermute x2 -> x3, waiting for transfers between devices: 14.1 us -> 11.2 us  [swapped(): return lax.ppermute(value, axis, pairs)]
    pallas_call x0 -> x2, Pallas kernels: none -> 2.75 us  [the longest x1 1.81 us: local(): call(bind(second_last_kernel, states - 1, len(parts_of(width)) - 1, legs,...]
    pallas_call x2 -> x1, Pallas kernels: 4.48 us -> 2.24 us  [local(): call(bind(second_kernel, group, legs, width), 'second_absorption', [(boun...]
    ppermute x2 -> x3, starting transfers between devices: 12.4 us -> 14.3 us  [swapped(): return lax.ppermute(value, axis, pairs)]
  transfers between devices with their start and end apart: 3 -> 4, of which waited for: 2 -> 3; matrix products, arithmetic and copies ran while one was open for 0% -> 0% of each run, Pallas kernels for 17% -> 20%
where the time goes in v5:
time: 46.1 us; the launch traced here: 45.8 us
  starting transfers between devices  19.7 us (43%)
  Pallas kernels  14.1 us (31%)
  waiting for transfers between devices  11.2 us (24%)
  other arithmetic  0.77 us (2%)
    ppermute x3, starting transfers between devices, swapped(): return lax.ppermute(value, axis, pairs)  14.3 us
    ppermute x3, waiting for transfers between devices, swapped(): return lax.ppermute(value, axis, pairs)  11.2 us
    ppermute x1, starting transfers between devices, passed_along(): return lax.ppermute(value, axis, pairs)  5.39 us
    pallas_call x1, Pallas kernels, local(): call(bind(prepare_first_kernel, every, legs, width), 'prepare_first', giv...  3.36 us
    pallas_call x1, Pallas kernels, local(): call(bind(first_kernel, every, legs, width), 'first_absorption', [((width...  3.25 us
    pallas_call x1, Pallas kernels, local(): call(bind(prepare_second_kernel, every, legs, width), 'prepare_second', r...  2.34 us
    pallas_call x1, Pallas kernels, local(): call(bind(second_kernel, group, legs, width), 'second_absorption', [(boun...  2.24 us
    pallas_call x1, Pallas kernels, local(): call(bind(second_last_kernel, states - 1, len(parts_of(width)) - 1, legs,...  1.81 us
  transfers between devices with their start and end apart: 4, of which 3 were waited for; matrix products, arithmetic and copies ran while one was open for 0% of the time, Pallas kernels for 20%

profile of v5, /device:TPU:193, one launch (start us, length us, event | category | flops | bytes accessed | tf_op | source)
XLA Modules:
  0.0 45.8 jit_solution(289101121894367063)
XLA Ops:
  0.0 0.8 %pad_add_fusion = s32[2,1,1,194]{3,2,1,0:T(1,128)S(1)} fusion(s32[2,1,1,2]{3,2,1,0:T(1,128)} %rest_2_.5, s32[2,1,1,192]{3,2,1,0:T(1,128)} %rest_4_.3), kind=kLoop, calls=%fused_computation | loop fusion | flops 388 | bytes 3104 | tf_op jit(solution)/shard_map/concatenate | solution.py:357
  0.8 5.4 %collective-permute-start = (s32[2,1,1,194]{3,2,1,0:T(1,128)S(1)}, s32[2,1,1,194]{3,2,1,0:T(1,128)S(1)}, u32[]{:S(2)}, u32[]{:S(2)}) collective-permute-start(s32[2,1,1,194]{3,2,1,0:T(1,128)S(1)} %pad_add_fusion), channel_id=1, source_target_pairs={{0,1},{1,2},{2,3},{3,4},{4,5},{5,6},{6,7},{7,0},{8,9},{9,10},{10,1... | collective-permute-start | bytes 4664 | tf_op jit(solution)/shard_map/ppermute | solution.py:19
  6.2 3.4 %prepare_first.1 = (bf16[2,192,768]{2,1,0:T(8,128)(2,1)S(1)}, s32[2,1,1,192]{3,2,1,0:T(1,128)S(1)}, s32[2,8,128]{2,1,0:T(8,128)S(1)}, bf16[768,192]{1,0:T(8,128)...) custom-call(s32[1,1,2]{2,1,0:T(1,128)} %bitcast.1, ...), custom_call_target="tpu_custom_call" | custom-call | flops 471859200 | bytes 1179648 | tf_op jit(solution)/shard_map/prepare_first/pallas_call | solution.py:397
  9.5 0.0 collective-permute-done.from_left_ref
  9.5 3.3 %first_absorption.1 = (bf16[192,768]{1,0:T(8,128)(2,1)S(1)}, bf16[192,768]{1,0:T(8,128)(2,1)S(1)}) custom-call(s32[2,1,1,194]{3,2,1,0:T(1,128)S(1)} %collective-permute-done.from_left_ref, bf16[2,192,768]{2,1,0:T(8,128)(2,1)S(1)} %get-tuple-element.33.given_ref, s32[2,1,1,192]{3,2,1,0:T(1,128)S(1)} %get-tuple-element.31.charge_ref, ...), custom_call_target="tpu_custom_call" | custom-call | flops 471859200 | bytes 1179648 | tf_op jit(solution)/shard_map/first_absorption/pallas_call | solution.py:401
  12.8 2.0 %collective-permute-start.3 = (bf16[192,768]{1,0:T(8,128)(2,1)S(1)}, bf16[192,768]{1,0:T(8,128)(2,1)S(1)}, u32[]{:S(2)}, u32[]{:S(2)}) collective-permute-start(bf16[192,768]{1,0:T(8,128)(2,1)S(1)} %get-tuple-element.41._after), channel_id=1, source_target_pairs={{0,8},{8,0},{16,24},{24,16},{32,40},{40,32},{48,56},{56,48},{64,72... | collective-permute-start | bytes 884744 | tf_op jit(solution)/shard_map/ppermute | solution.py:25
  14.8 0.1 first_absorption_rest.1
  14.9 10.4 %collective-permute-start.2 = (bf16[192,512]{1,0:T(8,128)(2,1)S(1)}, bf16[192,512]{1,0:T(8,128)(2,1)S(1)}, u32[]{:S(2)}, u32[]{:S(2)}) collective-permute-start(bf16[192,512]{1,0:T(8,128)(2,1)S(1)} %get-tuple-element.43._after), channel_id=1, source_target_pairs={{0,8},{8,0},{16,24},{24,16},{32,40},{40,32},{48,56},{56,48},{64,72... | collective-permute-start | bytes 589832 | tf_op jit(solution)/shard_map/ppermute | solution.py:25
  25.4 2.3 %prepare_second.1 = (bf16[768,192]{1,0:T(8,128)(2,1)S(1)}, bf16[256,256]{1,0:T(8,128)(2,1)S(1)}, bf16[768,192]{1,0:T(8,128)(2,1)S(1)}, bf16[768,192]{1,0:T(8,128...) custom-call(s32[2,1,1,194]{3,2,1,0:T(1,128)S(1)} %collective-permute-done.from_left_ref, ...), custom_call_target="tpu_custom_call" | custom-call | flops 471859200 | bytes 1179648 | tf_op jit(solution)/shard_map/prepare_second/pallas_call | solution.py:413
  27.7 1.9 %collective-permute-start.1 = (bf16[192,256]{1,0:T(8,128)(2,1)S(1)}, bf16[192,256]{1,0:T(8,128)(2,1)S(1)}, u32[]{:S(2)}, u32[]{:S(2)}) collective-permute-start(bf16[192,256]{1,0:T(8,128)(2,1)S(1)} %get-tuple-element.50), channel_id=1, source_target_pairs={{0,8},{8,0},{16,24},{24,16},{32,40},{40,32},{48,56},{56,48},{64,72... | collective-permute-start | bytes 294920 | tf_op jit(solution)/shard_map/ppermute | solution.py:25
  29.6 9.7 %collective-permute-done.3.rest_0_ = bf16[192,768]{1,0:T(8,128)(2,1)S(1)} collective-permute-done((bf16[192,768]{1,0:T(8,128)(2,1)S(1)}, bf16[192,768]{1,0:T(8,128)(2,1)S(1)}, u32[]{:S(2)}, u32[]{:S(2)}) %collective-permute-start.3) | collective-permute-done | bytes 294944 | tf_op jit(solution)/shard_map/ppermute | solution.py:25
  39.4 2.2 %second_absorption.1.rest_3_._out = bf16[2,1,1,192,768]{4,3,2,1,0:T(8,128)(2,1)} custom-call(bf16[192,768]{1,0:T(8,128)(2,1)S(1)} %collective-permute-done.3.rest_0_, bf16[768,192]{1,0:T(8,128)(2,1)S(1)} %get-tuple-element.54.rest_1_, bf16[256,256]{1,0:T(8,128)(2,1)S(1)} %get-tuple-element.55.rest_2_, bf16[768,192]{1,0:T(8,128)(2,1)S(1)} %get-tuple-element.56.rest_3_), custom_call_target="tpu_custom_call" | custom-call | flops 471859200 | bytes 1179648 | tf_op jit(solution)/shard_map/second_absorption/pallas_call | solution.py:424
  41.6 1.3 %collective-permute-done.2.received_ref = bf16[192,512]{1,0:T(8,128)(2,1)S(1)} collective-permute-done((bf16[192,512]{1,0:T(8,128)(2,1)S(1)}, bf16[192,512]{1,0:T(8,128)(2,1)S(1)}, u32[]{:S(2)}, u32[]{:S(2)}) %collective-permute-start.2) | collective-permute-done | bytes 196640 | tf_op jit(solution)/shard_map/ppermute | solution.py:25
  42.9 0.9 %second_absorption_part.1.total_ref = f32[4,192,192]{2,1,0:T(8,128)S(1)} custom-call(bf16[192,512]{1,0:T(8,128)(2,1)S(1)} %collective-permute-done.2.received_ref, bf16[768,192]{1,0:T(8,128)(2,1)S(1)} %get-tuple-element.51.rest_0_.stack_ref, bf16[256,256]{1,0:T(8,128)(2,1)S(1)} %get-tuple-element.52.rest_1_.kron_ref, ...), custom_call_target="tpu_custom_call" | custom-call | flops 471859200 | bytes 1179648 | tf_op jit(solution)/shard_map/second_absorption_part/pallas_call | solution.py:438
  43.9 0.1 collective-permute-done.1.received_ref
  44.0 1.8 %second_absorption_last.1 = bf16[2,1,1,192,768]{4,3,2,1,0:T(8,128)(2,1)} custom-call(bf16[192,256]{1,0:T(8,128)(2,1)S(1)} %collective-permute-done.1.received_ref, bf16[768,192]{1,0:T(8,128)(2,1)S(1)} %get-tuple-element.51.rest_0_.stack_ref, bf16[256,256]{1,0:T(8,128)(2,1)S(1)} %get-tuple-element.52.rest_1_.kron_ref, ...), custom_call_target="tpu_custom_call", output_to_operand_aliasing={{}: (5, {})} | custom-call | flops 471859200 | bytes 1179648 | tf_op jit(solution)/shard_map/second_absorption_last/pallas_call | solution.py:443
Async XLA Ops:
  0.8 8.8 %collective-permute-start = (s32[2,1,1,194]{3,2,1,0:T(1,128)S(1)}, s32[2,1,1,194]{3,2,1,0:T(1,128)S(1)}, u32[]{:S(2)}, u32[]{:S(2)}) collective-permute-start(s32[2,1,1,194]{3,2,1,0:T(1,128)S(1)} %pad_add_fusion), channel_id=1, source_target_pairs={{0,1},{1,2},{2,3},{3,4},{4,5},{5,6},{6,7},{7,0},{8,9},{9,10},{10,1... | collective-permute-start | bytes 4664 | tf_op jit(solution)/shard_map/ppermute | solution.py:19
  12.8 26.6 %collective-permute-start.3 = (bf16[192,768]{1,0:T(8,128)(2,1)S(1)}, bf16[192,768]{1,0:T(8,128)(2,1)S(1)}, u32[]{:S(2)}, u32[]{:S(2)}) collective-permute-start(bf16[192,768]{1,0:T(8,128)(2,1)S(1)} %get-tuple-element.41._after), channel_id=1, source_target_pairs={{0,8},{8,0},{16,24},{24,16},{32,40},{40,32},{48,56},{56,48},{64,72... | collective-permute-start | bytes 884744 | tf_op jit(solution)/shard_map/ppermute | solution.py:25
  14.9 28.0 %collective-permute-start.2 = (bf16[192,512]{1,0:T(8,128)(2,1)S(1)}, bf16[192,512]{1,0:T(8,128)(2,1)S(1)}, u32[]{:S(2)}, u32[]{:S(2)}) collective-permute-start(bf16[192,512]{1,0:T(8,128)(2,1)S(1)} %get-tuple-element.43._after), channel_id=1, source_target_pairs={{0,8},{8,0},{16,24},{24,16},{32,40},{40,32},{48,56},{56,48},{64,72... | collective-permute-start | bytes 589832 | tf_op jit(solution)/shard_map/ppermute | solution.py:25
  27.7 16.3 %collective-permute-start.1 = (bf16[192,256]{1,0:T(8,128)(2,1)S(1)}, bf16[192,256]{1,0:T(8,128)(2,1)S(1)}, u32[]{:S(2)}, u32[]{:S(2)}) collective-permute-start(bf16[192,256]{1,0:T(8,128)(2,1)S(1)} %get-tuple-element.50), channel_id=1, source_target_pairs={{0,8},{8,0},{16,24},{24,16},{32,40},{40,32},{48,56},{56,48},{64,72... | collective-permute-start | bytes 294920 | tf_op jit(solution)/shard_map/ppermute | solution.py:25
